TPU v7x, 128 devices: a whole 4x4x4 slice. The times are simulated.
128 devices in a mesh: dp: 8 (over z_lo, y), ctx: 16 (over z_hi, x, core).
Axes of the slice: x: 4, y: 4, z: 4 (z_hi: 2, z_lo: 2; z = z_hi * 2 + z_lo), core: 2. Of those that a mesh axis runs over, the one named last changes fastest.
Arguments:
- tokens: float32 [8, 2048, 768], P('dp', 'ctx'), may hold values from -6 to 6
- cotangent: float32 [8, 2048, 768], P('dp', 'ctx'), may hold values from -6 to 6
- w_qkv: bfloat16 [1, 768, 2304], P(None, ('dp', 'ctx')), may hold values from -0.21875 to 0.21875
- w_out: bfloat16 [1, 768, 768], P(None, ('dp', 'ctx')), may hold values from -0.875 to 0.875
- w_fc: bfloat16 [1, 768, 3072], P(None, ('dp', 'ctx')), may hold values from -0.21875 to 0.21875
- w_proj: bfloat16 [1, 3072, 768], P(None, ('dp', 'ctx')), may hold values from -0.109375 to 0.109375
- gains: bfloat16 [1, 2, 768], P(None, None, ('dp', 'ctx')), may hold values from 0.5 to 1.5
- biases: bfloat16 [1, 6, 768], P(None, None, ('dp', 'ctx')), may hold values from -2 to 2
- fc_bias: bfloat16 [1, 3072], P(None, ('dp', 'ctx')), may hold values from -2 to 2
Outputs:
- final: float32 [8, 2048, 768], P('dp', 'ctx')
- input_grad: float32 [8, 2048, 768], P('dp', 'ctx')
- grad_qkv: float32 [1, 768, 2304], P(None, ('dp', 'ctx'))
- grad_out: float32 [1, 768, 768], P(None, ('dp', 'ctx'))
- grad_fc: float32 [1, 768, 3072], P(None, ('dp', 'ctx'))
- grad_proj: float32 [1, 3072, 768], P(None, ('dp', 'ctx'))
- grad_gains: float32 [1, 2, 768], P(None, None, ('dp', 'ctx'))
- grad_biases: float32 [1, 6, 768], P(None, None, ('dp', 'ctx'))
- grad_fc_bias: float32 [1, 3072], P(None, ('dp', 'ctx'))
All inputs are finite; a program needn't handle non-finite values.
Results may differ from a plain program's by a relative error of at most 0.025.
Values may be sent and summed in bfloat16 or wider, within the bound.
A program may use at most 128 MiB of HBM per device.

v0:
```python
import jax
import jax.numpy as jnp
from jax import lax
from jax.sharding import PartitionSpec as P

HEAD = 64


norm_eps = 1e-05
masked_score = -1e30


def from_behind(block, axis, distance):
    devices = range(lax.axis_size(axis))
    route = [((i - distance) % len(devices), i) for i in devices]
    return lax.ppermute(block, axis, route)


def row_positions(rows, block_len, axis_len):
    part = rows // block_len
    offset = rows % block_len
    half = block_len // 2
    return jnp.where(
        offset < half, part * half + offset, (2 * axis_len - 1 - part) * half + offset - half
    )


def block_positions(block_idx, block_len, axis_len):
    rows = block_idx * block_len + jnp.arange(block_len, dtype=jnp.int32)
    return row_positions(rows, block_len, axis_len)


def layer_norm(values, gain, offset):
    center = values - jnp.mean(values, axis=-1, keepdims=True)
    spread = jnp.mean(center * center, axis=-1, keepdims=True)
    return center * lax.rsqrt(spread + norm_eps) * gain + offset


def gelu_tanh(values):
    return jax.nn.gelu(values, approximate=True)


def rows_product(left, right):
    return lax.dot_general(
        left, right, (((0,), (0,)), ((), ())), preferred_element_type=jnp.float32
    )


def back_product(left, right):
    return lax.dot_general(
        left, right, (((1,), (1,)), ((), ())), preferred_element_type=jnp.float32
    )


def block_setup(query, keys, values):
    seqs_here, block_len, heads, head_dim = query.shape
    width = heads * head_dim
    packed = jnp.concatenate(
        [keys.reshape(seqs_here, block_len, width), values.reshape(seqs_here, block_len, width)],
        axis=2,
    )
    my_block = lax.axis_index("ctx")
    query_pos = block_positions(my_block, block_len, lax.axis_size("ctx"))
    return (packed, my_block, query_pos)


def unpack_block(packed, shape_four):
    width = packed.shape[2] // 2
    return (packed[:, :, :width].reshape(shape_four), packed[:, :, width:].reshape(shape_four))


def stepped_forward(query, keys, values):
    seqs_here, block_len, heads, head_dim = query.shape
    axis_len = lax.axis_size("ctx")
    scale = head_dim ** (-0.5)
    packed, my_block, query_pos = block_setup(query, keys, values)

    def absorb(carry, packed, step_idx):
        best, total, accum = carry
        key_block, value_block = unpack_block(packed, query.shape)
        owner = (my_block - step_idx) % axis_len
        key_pos = block_positions(owner, block_len, axis_len)
        allowed = query_pos[:, None] >= key_pos[None, :]
        scores = (
            jnp.einsum("sqhd,skhd->shqk", query, key_block, preferred_element_type=jnp.float32)
            * scale
        )
        scores = jnp.where(allowed, scores, masked_score)
        new_best = jnp.maximum(best, jnp.max(scores, axis=-1))
        fade = jnp.exp(best - new_best)
        exp_scores = jnp.exp(scores - new_best[..., None])
        total = total * fade + jnp.sum(exp_scores, axis=-1)
        update = jnp.einsum(
            "shqk,skhd->sqhd",
            exp_scores.astype(jnp.bfloat16),
            value_block,
            preferred_element_type=jnp.float32,
        )
        accum = accum * jnp.transpose(fade, (0, 2, 1))[..., None] + update
        return (new_best, total, accum)

    start = (
        jnp.full((seqs_here, heads, block_len), masked_score, jnp.float32),
        jnp.zeros((seqs_here, heads, block_len), jnp.float32),
        jnp.zeros(query.shape, jnp.float32),
    )
    carry = absorb(start, packed, 0)

    def turn(step_idx, state):
        moving, inner = state
        moving = from_behind(moving, "ctx", 1)
        return (moving, absorb(inner, moving, step_idx))

    packed, carry = lax.fori_loop(1, axis_len, turn, (packed, carry))
    best, total, accum = carry
    output = accum / jnp.transpose(total, (0, 2, 1))[..., None]
    return (output, best + jnp.log(total), None)


def stepped_backward(query, keys, values, grad_attn, output, log_total):
    seqs_here, block_len, heads, head_dim = query.shape
    width = heads * head_dim
    axis_len = lax.axis_size("ctx")
    scale = head_dim ** (-0.5)
    packed, my_block, query_pos = block_setup(query, keys, values)
    delta = jnp.transpose(jnp.sum(grad_attn.astype(jnp.float32) * output, axis=-1), (0, 2, 1))

    def absorb(grad_query, grad_packed, packed, step_idx):
        key_block, value_block = unpack_block(packed, query.shape)
        owner = (my_block - step_idx) % axis_len
        key_pos = block_positions(owner, block_len, axis_len)
        allowed = query_pos[:, None] >= key_pos[None, :]
        scores = (
            jnp.einsum("sqhd,skhd->shqk", query, key_block, preferred_element_type=jnp.float32)
            * scale
        )
        prob = jnp.exp(jnp.where(allowed, scores - log_total[..., None], masked_score))
        dprob = jnp.einsum(
            "sqhd,skhd->shqk", grad_attn, value_block, preferred_element_type=jnp.float32
        )
        dscore = (prob * (dprob - delta[..., None])).astype(jnp.bfloat16)
        grad_query = (
            grad_query
            + jnp.einsum("shqk,skhd->sqhd", dscore, key_block, preferred_element_type=jnp.float32)
            * scale
        )
        grad_keys = (
            jnp.einsum("shqk,sqhd->skhd", dscore, query, preferred_element_type=jnp.float32) * scale
        )
        grad_values = jnp.einsum(
            "shqk,sqhd->skhd",
            prob.astype(jnp.bfloat16),
            grad_attn,
            preferred_element_type=jnp.float32,
        )
        grad_packed = grad_packed + jnp.concatenate(
            [
                grad_keys.reshape(seqs_here, block_len, width),
                grad_values.reshape(seqs_here, block_len, width),
            ],
            axis=2,
        )
        return (grad_query, grad_packed)

    grad_query, grad_packed = absorb(
        jnp.zeros(query.shape, jnp.float32),
        jnp.zeros((seqs_here, block_len, 2 * width), jnp.float32),
        packed,
        0,
    )

    def turn(step_idx, state):
        moving, grad_q, grad_p = state
        moving = from_behind(moving, "ctx", 1)
        grad_p = from_behind(grad_p.astype(jnp.bfloat16), "ctx", 1).astype(grad_p.dtype)
        grad_q, grad_p = absorb(grad_q, grad_p, moving, step_idx)
        return (moving, grad_q, grad_p)

    packed, grad_query, grad_packed = lax.fori_loop(
        1, axis_len, turn, (packed, grad_query, grad_packed)
    )
    grad_packed = from_behind(grad_packed.astype(jnp.bfloat16), "ctx", 1).astype(grad_packed.dtype)
    return (grad_query, grad_packed[:, :, :width], grad_packed[:, :, width:])


def fetch_layer(w_qkv, w_out, w_fc, w_proj, gains, biases, fc_bias, layer_idx):
    return (
        lax.all_gather(w_qkv[layer_idx], ("dp", "ctx"), axis=0, tiled=True),
        lax.all_gather(w_out[layer_idx], ("dp", "ctx"), axis=0, tiled=True),
        lax.all_gather(w_fc[layer_idx], ("dp", "ctx"), axis=0, tiled=True),
        lax.all_gather(w_proj[layer_idx], ("dp", "ctx"), axis=0, tiled=True),
        lax.all_gather(gains[layer_idx], ("dp", "ctx"), axis=1, tiled=True),
        lax.all_gather(biases[layer_idx], ("dp", "ctx"), axis=1, tiled=True),
        lax.all_gather(fc_bias[layer_idx], ("dp", "ctx"), axis=0, tiled=True),
    )


def forward_layer(tok_rows, gathered, shape_four):
    mat_qkv, mat_out, mat_fc, mat_proj, gain_pair, bias_six, hidden_bias = gathered
    width = tok_rows.shape[1]
    gain_pair = gain_pair.astype(jnp.float32)
    bias_six = bias_six.astype(jnp.float32)
    normed_one = layer_norm(tok_rows, gain_pair[0], bias_six[0]).astype(jnp.bfloat16)
    projected = jnp.dot(normed_one, mat_qkv, preferred_element_type=jnp.float32)
    query = (projected[:, :width] + bias_six[1]).astype(jnp.bfloat16).reshape(shape_four)
    keys = projected[:, width : 2 * width].astype(jnp.bfloat16).reshape(shape_four)
    values = (projected[:, 2 * width :] + bias_six[2]).astype(jnp.bfloat16).reshape(shape_four)
    output, log_total, whole = stepped_forward(query, keys, values)
    attended = output.reshape(tok_rows.shape).astype(jnp.bfloat16)
    middle = tok_rows + jnp.dot(attended, mat_out, preferred_element_type=jnp.float32) + bias_six[3]
    normed_two = layer_norm(middle, gain_pair[1], bias_six[4]).astype(jnp.bfloat16)
    hidden_pre = jnp.dot(
        normed_two, mat_fc, preferred_element_type=jnp.float32
    ) + hidden_bias.astype(jnp.float32)
    activated = gelu_tanh(hidden_pre).astype(jnp.bfloat16)
    result = middle + jnp.dot(activated, mat_proj, preferred_element_type=jnp.float32) + bias_six[5]
    saved = (
        tok_rows,
        normed_one,
        query,
        keys,
        values,
        output,
        log_total,
        attended,
        middle,
        normed_two,
        hidden_pre,
        activated,
        whole,
    )
    return (result, saved)


def backward_layer(gradient, gathered, saved):
    mat_qkv, mat_out, mat_fc, mat_proj, gain_pair, bias_six, hidden_bias = gathered
    (
        tok_rows,
        normed_one,
        query,
        keys,
        values,
        output,
        log_total,
        attended,
        middle,
        normed_two,
        hidden_pre,
        activated,
        whole,
    ) = saved
    gain_pair = gain_pair.astype(jnp.float32)
    bias_six = bias_six.astype(jnp.float32)
    d_two = gradient.astype(jnp.bfloat16)
    grad_proj = rows_product(activated, d_two)
    grad_bias_five = jnp.sum(d_two.astype(jnp.float32), axis=0)
    d_act = back_product(d_two, mat_proj)
    gelu_back = jax.vjp(gelu_tanh, hidden_pre)[1]
    d_pre = gelu_back(d_act)[0].astype(jnp.bfloat16)
    grad_hidden_bias = jnp.sum(d_pre.astype(jnp.float32), axis=0)
    grad_fc = rows_product(normed_two, d_pre)
    d_norm_two = back_product(d_pre, mat_fc)
    norm_back_two = jax.vjp(layer_norm, middle, gain_pair[1], bias_six[4])[1]
    d_mid_part, grad_gain_two, grad_bias_four = norm_back_two(d_norm_two)
    d_middle = gradient + d_mid_part
    d_one = d_middle.astype(jnp.bfloat16)
    grad_out = rows_product(attended, d_one)
    grad_bias_three = jnp.sum(d_one.astype(jnp.float32), axis=0)
    d_attended = back_product(d_one, mat_out).astype(jnp.bfloat16).reshape(query.shape)
    grad_query, grad_keys, grad_values = stepped_backward(
        query, keys, values, d_attended, output, log_total
    )
    grad_query = grad_query.reshape(tok_rows.shape).astype(jnp.bfloat16)
    grad_keys = grad_keys.reshape(tok_rows.shape).astype(jnp.bfloat16)
    grad_values = grad_values.reshape(tok_rows.shape).astype(jnp.bfloat16)
    grad_bias_one = jnp.sum(grad_query.astype(jnp.float32), axis=0)
    grad_bias_two = jnp.sum(grad_values.astype(jnp.float32), axis=0)
    grad_joint = jnp.concatenate([grad_query, grad_keys, grad_values], axis=1)
    grad_qkv = rows_product(normed_one, grad_joint)
    d_norm_one = back_product(grad_joint, mat_qkv)
    norm_back_one = jax.vjp(layer_norm, tok_rows, gain_pair[0], bias_six[0])[1]
    d_rows_part, grad_gain_one, grad_bias_zero = norm_back_one(d_norm_one)
    d_input = d_middle + d_rows_part
    grad_gain_pair = jnp.stack([grad_gain_one, grad_gain_two])
    grad_bias_six = jnp.stack(
        [
            grad_bias_zero,
            grad_bias_one,
            grad_bias_two,
            grad_bias_three,
            grad_bias_four,
            grad_bias_five,
        ]
    )
    return (
        d_input,
        (grad_qkv, grad_out, grad_fc, grad_proj, grad_gain_pair, grad_bias_six, grad_hidden_bias),
    )


def local(tokens, cotangent, w_qkv, w_out, w_fc, w_proj, gains, biases, fc_bias):
    seqs_here, block_len, width = tokens.shape
    layer_count = w_qkv.shape[0]
    shape_four = (seqs_here, block_len, width // HEAD, HEAD)
    state = tokens.reshape(seqs_here * block_len, width)
    layer_idx = 0
    gathered = fetch_layer(w_qkv, w_out, w_fc, w_proj, gains, biases, fc_bias, layer_idx)
    state, saved = forward_layer(state, gathered, shape_four)
    kept_weights = [gathered]
    kept_saved = [saved]
    final = state.reshape(tokens.shape)
    gradient = cotangent.reshape(seqs_here * block_len, width)
    results = [None] * layer_count
    for layer_idx in reversed(range(layer_count)):
        gathered = kept_weights[layer_idx]
        gradient, partial_grads = backward_layer(gradient, gathered, kept_saved[layer_idx])
        results[layer_idx] = (
            lax.psum_scatter(partial_grads[0], ("dp", "ctx"), scatter_dimension=0, tiled=True),
            lax.psum_scatter(partial_grads[1], ("dp", "ctx"), scatter_dimension=0, tiled=True),
            lax.psum_scatter(partial_grads[2], ("dp", "ctx"), scatter_dimension=0, tiled=True),
            lax.psum_scatter(partial_grads[3], ("dp", "ctx"), scatter_dimension=0, tiled=True),
            lax.psum_scatter(partial_grads[4], ("dp", "ctx"), scatter_dimension=1, tiled=True),
            lax.psum_scatter(partial_grads[5], ("dp", "ctx"), scatter_dimension=1, tiled=True),
            lax.psum_scatter(partial_grads[6], ("dp", "ctx"), scatter_dimension=0, tiled=True),
        )
    stacked = [jnp.stack([results[0][member]]) for member in range(7)]
    return (
        final,
        gradient.reshape(tokens.shape),
        stacked[0],
        stacked[1],
        stacked[2],
        stacked[3],
        stacked[4],
        stacked[5],
        stacked[6],
    )


def solution(mesh):
    in_specs = (
        P("dp", "ctx", None),
        P("dp", "ctx", None),
        P(None, ("dp", "ctx"), None),
        P(None, ("dp", "ctx"), None),
        P(None, ("dp", "ctx"), None),
        P(None, ("dp", "ctx"), None),
        P(None, None, ("dp", "ctx")),
        P(None, None, ("dp", "ctx")),
        P(None, ("dp", "ctx")),
    )
    out_specs = (
        P("dp", "ctx", None),
        P("dp", "ctx", None),
        P(None, ("dp", "ctx"), None),
        P(None, ("dp", "ctx"), None),
        P(None, ("dp", "ctx"), None),
        P(None, ("dp", "ctx"), None),
        P(None, None, ("dp", "ctx")),
        P(None, None, ("dp", "ctx")),
        P(None, ("dp", "ctx")),
    )
    return jax.shard_map(local, mesh=mesh, in_specs=in_specs, out_specs=out_specs, check_vma=False)
```

profile of v0, /device:TPU:1, one launch (start us, length us, event | category | flops | bytes accessed | tf_op | source)
XLA Modules:
  0.0 2010.8 jit_solution(17318551123252139060)
XLA Ops:
  13.1 181.1 %all-gather.1 = bf16[1,6,768]{1,0,2:T(2,128)(2,1)S(1)} all-gather(bf16[1,6,6]{1,0,2:T(2,128)(2,1)S(1)} %copy.85), channel_id=3, replica_groups=mesh['dp'=8,'ctx'=16] {'dp','ctx'}, dimensions={2}, use_global_device_ids=true | all-gather | bytes 9288 | tf_op jit(solution)/shard_map/all_gather | solution.py:193
  208.2 172.0 %all-gather = bf16[1,2,768]{1,0,2:T(2,128)(2,1)S(1)} all-gather(bf16[1,2,6]{1,0,2:T(2,128)(2,1)S(1)} %copy.84), channel_id=2, replica_groups=mesh['dp'=8,'ctx'=16] {'dp','ctx'}, dimensions={2}, use_global_device_ids=true | all-gather | bytes 3096 | tf_op jit(solution)/shard_map/all_gather | solution.py:192
  386.4 62.8 %all-reduce = bf16[3072]{0:T(1024)(128)(2,1)S(1)} all-reduce(bf16[3072]{0:T(1024)(128)(2,1)S(1)} %dynamic-update-slice), channel_id=7, replica_groups=mesh['dp'=8,'ctx'=16] {'dp','ctx'}, use_global_device_ids=true, to_apply=%add | all-reduce | flops 3072 | bytes 12288
  455.5 169.2 %while.44 = (s32[]{:T(128)}, bf16[1,128,1536]{1,2,0:T(8,128)(2,1)S(1)}, f32[1,12,128]{2,1,0:T(8,128)S(1)}, f32[1,12,128]{2,1,0:T(8,128)S(1)}, f32[1,128,12,64]{1...) while((s32[]{:T(128)}, ...), condition=%wide.region_7.8_spmd.clone, body=%wide.region_4.7_spmd.clone.sunk | while | flops 51932688 | bytes 7014706 | solution.py:114
  627.7 39.7 %all-gather.16.cloned.1.call-done = bf16[1,768,3072]{2,0,1:T(2,128)(2,1)} async-done(((bf16[1,6,3072]{2,0,1:T(2,128)(2,1)}), bf16[1,768,3072]{2,0,1:T(2,128)(2,1)}) %all-gather.16.cloned.1.call-update) | async-done | bytes 4718608 | tf_op jit(solution)/shard_map/all_gather | solution.py:190
  674.1 193.1 %all-gather.18.cloned.1.call-done = bf16[1,3072,768]{2,1,0:T(8,128)(2,1)} async-done(((bf16[1,24,768]{2,1,0:T(8,128)(2,1)}), bf16[1,3072,768]{2,1,0:T(8,128)(2,1)}) %all-gather.18.cloned.1.call-update) | async-done | bytes 4718608 | tf_op jit(solution)/shard_map/all_gather | solution.py:191
  890.4 242.1 %while.45 = (s32[]{:T(128)}, bf16[1,128,1536]{1,2,0:T(8,128)(2,1)S(1)}, f32[1,128,12,64]{1,3,2,0:T(8,128)S(1)}, bf16[1,128,1536]{1,2,0:T(8,128)(2,1)}, s32[]{:T(...) while((s32[]{:T(128)}, ...), condition=%wide.region_14.15_spmd.clone, body=%wide.region_13.14_spmd.clone.sunk | while | flops 128310288 | bytes 12826986 | solution.py:179
  947.4 14.3 collective-permute-done.1
  964.5 13.9 collective-permute-done.1
  981.1 14.1 collective-permute-done.1
  997.9 14.0 collective-permute-done.1
  1014.7 14.1 collective-permute-done.1
  1031.6 14.3 collective-permute-done.1
  1048.6 14.2 collective-permute-done.1
  1065.5 13.9 collective-permute-done.1
  1082.2 14.0 collective-permute-done.1
  1099.0 14.1 collective-permute-done.1
  1115.8 14.1 collective-permute-done.1
  1152.5 376.9 %fusion.107 = (f32[8,2304]{1,0:T(8,128)}, f32[8,768]{1,0:T(8,128)}, f32[8,3072]{1,0:T(8,128)}) fusion(f32[768,2304]{1,0:T(8,128)} %fusion.92, f32[768,768]{1,0:T(8,128)S(1)} %fusion.119, f32[768,3072]{1,0:T(8,128)} %fusion.104), kind=kCustom, calls=%all-reduce-scatter.3 | all-reduce-scatter fusion | flops 6291457 | bytes 19070976
  1542.0 16.2 collective-permute-start.58
  1727.8 72.1 %all-reduce.10 = (f32[2,768]{1,0:T(2,128)S(1)}, f32[6,768]{1,0:T(8,128)S(1)}, f32[3072]{0:T(1024)S(1)}) all-reduce(f32[2,768]{1,0:T(2,128)S(1)} %pad_maximum_fusion.5, f32[6,768]{1,0:T(8,128)S(1)} %stack.53, f32[3072]{0:T(1024)S(1)} %copy-done.115), channel_id=13, replica_groups=mesh['dp'=8,'ctx'=16] {'dp','ctx'}, use_global_device_ids=true, to_apply=%region_23.24.clone | all-reduce | flops 9216 | bytes 73728
  1854.0 26.5 %concatenate.26 = f32[262,768]{1,0:T(8,128)S(1)} concatenate(f32[6,768]{1,0:T(8,128)S(1)} %collective-permute-done.67, f32[8,768]{1,0:T(8,128)} %copy-done.87, f32[8,768]{1,0:T(8,128)} %copy-done.88, f32[8,768]{1,0:T(8,128)} %copy-done.89, f32[8,768]{1,0:T(8,128)} %copy-done.90, f32[8,768]{1,0:T(8,128)} %copy-done.91, f32[8,768]{1,0:T(8,128)} %copy-done.92, f32[8,768]{1,0:T(8,128)} %copy-done.93, ...), dimensions={0} | concatenate | bytes 1609728
  1897.4 31.7 %concatenate.25 = f32[262,2304]{1,0:T(8,128)S(1)} concatenate(f32[6,2304]{1,0:T(8,128)} %copy-done.58, f32[8,2304]{1,0:T(8,128)S(1)} %copy-done.55, f32[8,2304]{1,0:T(8,128)} %copy-done.56, f32[8,2304]{1,0:T(8,128)} %copy-done.57, f32[8,2304]{1,0:T(8,128)} %copy-done.59, f32[8,2304]{1,0:T(8,128)} %copy-done.60, f32[8,2304]{1,0:T(8,128)} %copy-done.61, f32[8,2304]{1,0:T(8,128)} %copy-done.62, ...), dimensions={0} | concatenate | bytes 4829184
  1947.4 54.8 %concatenate.27 = f32[262,3072]{1,0:T(8,128)} concatenate(f32[6,3072]{1,0:T(8,128)S(1)} %collective-permute-done.99, f32[8,3072]{1,0:T(8,128)S(1)} %collective-permute-done.98, f32[8,3072]{1,0:T(8,128)S(1)} %collective-permute-done.97, f32[8,3072]{1,0:T(8,128)S(1)} %collective-permute-done.96, f32[8,3072]{1,0:T(8,128)S(1)} %collective-permute-done.95, ...), dimensions={0} | concatenate | bytes 6438912
  (964 shorter events, 609.0 us)
Async XLA Ops:
  7.2 442.7 %all-gather.12.cloned.1.call-start = ((), (), s32[]{:S(2)}) async-start(), calls=%async_computation.2 | async-start | bytes 7133184 | tf_op jit(solution)/shard_map/all_gather | solution.py:188
  8.7 616.0 %all-gather.14.cloned.1.call-start = ((), (), s32[]{:S(2)}) async-start(), calls=%async_computation.3 | async-start | bytes 2377728 | tf_op jit(solution)/shard_map/all_gather | solution.py:189
  10.1 657.3 %all-gather.16.cloned.1.call-start = ((), (), s32[]{:S(2)}) async-start(), calls=%async_computation.4 | async-start | bytes 9510912 | tf_op jit(solution)/shard_map/all_gather | solution.py:190
  11.6 855.6 %all-gather.18.cloned.1.call-start = ((), (), s32[]{:S(2)}) async-start(), calls=%async_computation.5 | async-start | bytes 4755456 | tf_op jit(solution)/shard_map/all_gather | solution.py:191
  12.2 1991.6 %reduce-scatter.10.cloned.1.call-start = ((), (), s32[]{:S(2)}) async-start(), calls=%async_computation.1 | async-start | bytes 9510912 | tf_op jit(solution)/shard_map/reduce_scatter | solution.py:321
  1538.0 22.8 %collective-permute-start.61 = (f32[8,768]{1,0:T(8,128)}, f32[8,768]{1,0:T(8,128)S(1)}, u32[]{:S(2)}, u32[]{:S(2)}) collective-permute-start(f32[8,768]{1,0:T(8,128)} %get-tuple-element.742), channel_id=1, source_target_pairs={{0,26},{1,27},{2,28},{3,29},{4,30},{5,31},{6,32},{7,33},{8,34},{9,... | collective-permute-start | bytes 73736
  1539.3 24.0 %collective-permute-start.60 = (f32[8,768]{1,0:T(8,128)}, f32[8,768]{1,0:T(8,128)S(1)}, u32[]{:S(2)}, u32[]{:S(2)}) collective-permute-start(f32[8,768]{1,0:T(8,128)} %get-tuple-element.742), channel_id=1, source_target_pairs={{0,25},{1,26},{2,27},{3,28},{4,29},{5,30},{6,31},{7,32},{8,33},{9,... | collective-permute-start | bytes 73736
  1540.6 24.9 %collective-permute-start.59 = (f32[8,768]{1,0:T(8,128)}, f32[8,768]{1,0:T(8,128)S(1)}, u32[]{:S(2)}, u32[]{:S(2)}) collective-permute-start(f32[8,768]{1,0:T(8,128)} %get-tuple-element.742), channel_id=1, source_target_pairs={{0,24},{1,25},{2,26},{3,27},{4,28},{5,29},{6,30},{7,31},{8,32},{9,... | collective-permute-start | bytes 73736
  1542.0 27.1 %collective-permute-start.58 = (f32[8,768]{1,0:T(8,128)}, f32[8,768]{1,0:T(8,128)S(1)}, u32[]{:S(2)}, u32[]{:S(2)}) collective-permute-start(f32[8,768]{1,0:T(8,128)} %get-tuple-element.742), channel_id=1, source_target_pairs={{0,23},{1,24},{2,25},{3,26},{4,27},{5,28},{6,29},{7,30},{8,31},{9,... | collective-permute-start | bytes 73736
  1714.9 85.0 %collective-permute-start.97 = (f32[8,3072]{1,0:T(8,128)S(1)}, f32[8,3072]{1,0:T(8,128)S(1)}, u32[]{:S(2)}, u32[]{:S(2)}) collective-permute-start(f32[8,3072]{1,0:T(8,128)S(1)} %copy-done.8), channel_id=1, source_target_pairs={{0,30},{1,31},{2,32},{3,33},{4,34},{5,35},{6,36},{7,37},{8,38},{9,... | collective-permute-start | bytes 294920
  1717.0 87.1 %collective-permute-start.96 = (f32[8,3072]{1,0:T(8,128)S(1)}, f32[8,3072]{1,0:T(8,128)S(1)}, u32[]{:S(2)}, u32[]{:S(2)}) collective-permute-start(f32[8,3072]{1,0:T(8,128)S(1)} %copy-done.8), channel_id=1, source_target_pairs={{0,29},{1,30},{2,31},{3,32},{4,33},{5,34},{6,35},{7,36},{8,37},{9,... | collective-permute-start | bytes 294920
  1718.7 90.3 %collective-permute-start.95 = (f32[8,3072]{1,0:T(8,128)S(1)}, f32[8,3072]{1,0:T(8,128)S(1)}, u32[]{:S(2)}, u32[]{:S(2)}) collective-permute-start(f32[8,3072]{1,0:T(8,128)S(1)} %copy-done.8), channel_id=1, source_target_pairs={{0,28},{1,29},{2,30},{3,31},{4,32},{5,33},{6,34},{7,35},{8,36},{9,... | collective-permute-start | bytes 294920
  1720.0 93.9 %collective-permute-start.94 = (f32[8,3072]{1,0:T(8,128)S(1)}, f32[8,3072]{1,0:T(8,128)S(1)}, u32[]{:S(2)}, u32[]{:S(2)}) collective-permute-start(f32[8,3072]{1,0:T(8,128)S(1)} %copy-done.8), channel_id=1, source_target_pairs={{0,27},{1,28},{2,29},{3,30},{4,31},{5,32},{6,33},{7,34},{8,35},{9,... | collective-permute-start | bytes 294920
  1721.9 94.4 %collective-permute-start.93 = (f32[8,3072]{1,0:T(8,128)S(1)}, f32[8,3072]{1,0:T(8,128)S(1)}, u32[]{:S(2)}, u32[]{:S(2)}) collective-permute-start(f32[8,3072]{1,0:T(8,128)S(1)} %copy-done.8), channel_id=1, source_target_pairs={{0,26},{1,27},{2,28},{3,29},{4,30},{5,31},{6,32},{7,33},{8,34},{9,... | collective-permute-start | bytes 294920
  1835.9 44.6 %collective-permute-start.82 = (f32[8,3072]{1,0:T(8,128)S(1)}, f32[8,3072]{1,0:T(8,128)S(1)}, u32[]{:S(2)}, u32[]{:S(2)}) collective-permute-start(f32[8,3072]{1,0:T(8,128)S(1)} %copy-done.8), channel_id=1, source_target_pairs={{0,15},{1,16},{2,17},{3,18},{4,19},{5,20},{6,21},{7,22},{8,23},{9,... | collective-permute-start | bytes 294920
  1837.2 46.9 %collective-permute-start.81 = (f32[8,3072]{1,0:T(8,128)S(1)}, f32[8,3072]{1,0:T(8,128)S(1)}, u32[]{:S(2)}, u32[]{:S(2)}) collective-permute-start(f32[8,3072]{1,0:T(8,128)S(1)} %copy-done.8), channel_id=1, source_target_pairs={{0,14},{1,15},{2,16},{3,17},{4,18},{5,19},{6,20},{7,21},{8,22},{9,... | collective-permute-start | bytes 294920
  1843.3 42.7 %collective-permute-start.80 = (f32[8,3072]{1,0:T(8,128)S(1)}, f32[8,3072]{1,0:T(8,128)S(1)}, u32[]{:S(2)}, u32[]{:S(2)}) collective-permute-start(f32[8,3072]{1,0:T(8,128)S(1)} %copy-done.8), channel_id=1, source_target_pairs={{0,13},{1,14},{2,15},{3,16},{4,17},{5,18},{6,19},{7,20},{8,21},{9,... | collective-permute-start | bytes 294920
  1844.7 45.7 %collective-permute-start.79 = (f32[8,3072]{1,0:T(8,128)S(1)}, f32[8,3072]{1,0:T(8,128)S(1)}, u32[]{:S(2)}, u32[]{:S(2)}) collective-permute-start(f32[8,3072]{1,0:T(8,128)S(1)} %copy-done.8), channel_id=1, source_target_pairs={{0,12},{1,13},{2,14},{3,15},{4,16},{5,17},{6,18},{7,19},{8,20},{9,... | collective-permute-start | bytes 294920
  1848.4 46.2 %collective-permute-start.78 = (f32[8,3072]{1,0:T(8,128)S(1)}, f32[8,3072]{1,0:T(8,128)S(1)}, u32[]{:S(2)}, u32[]{:S(2)}) collective-permute-start(f32[8,3072]{1,0:T(8,128)S(1)} %copy-done.8), channel_id=1, source_target_pairs={{0,11},{1,12},{2,13},{3,14},{4,15},{5,16},{6,17},{7,18},{8,19},{9,... | collective-permute-start | bytes 294920
  1880.5 48.6 %collective-permute-start.77 = (f32[8,3072]{1,0:T(8,128)S(1)}, f32[8,3072]{1,0:T(8,128)}, u32[]{:S(2)}, u32[]{:S(2)}) collective-permute-start(f32[8,3072]{1,0:T(8,128)S(1)} %copy-done.8), channel_id=1, source_target_pairs={{0,10},{1,11},{2,12},{3,13},{4,14},{5,15},{6,16},{7,17},{8,18},{9,... | collective-permute-start | bytes 294920
  1884.1 48.8 %collective-permute-start.76 = (f32[8,3072]{1,0:T(8,128)S(1)}, f32[8,3072]{1,0:T(8,128)}, u32[]{:S(2)}, u32[]{:S(2)}) collective-permute-start(f32[8,3072]{1,0:T(8,128)S(1)} %copy-done.8), channel_id=1, source_target_pairs={{0,9},{1,10},{2,11},{3,12},{4,13},{5,14},{6,15},{7,16},{8,17},{9,1... | collective-permute-start | bytes 294920
  1886.1 49.6 %collective-permute-start.75 = (f32[8,3072]{1,0:T(8,128)S(1)}, f32[8,3072]{1,0:T(8,128)}, u32[]{:S(2)}, u32[]{:S(2)}) collective-permute-start(f32[8,3072]{1,0:T(8,128)S(1)} %copy-done.8), channel_id=1, source_target_pairs={{0,8},{1,9},{2,10},{3,11},{4,12},{5,13},{6,14},{7,15},{8,16},{9,17... | collective-permute-start | bytes 294920
  1890.3 49.6 %collective-permute-start.74 = (f32[8,3072]{1,0:T(8,128)S(1)}, f32[8,3072]{1,0:T(8,128)}, u32[]{:S(2)}, u32[]{:S(2)}) collective-permute-start(f32[8,3072]{1,0:T(8,128)S(1)} %copy-done.8), channel_id=1, source_target_pairs={{0,7},{1,8},{2,9},{3,10},{4,11},{5,12},{6,13},{7,14},{8,15},{9,16}... | collective-permute-start | bytes 294920
  1894.7 47.5 %collective-permute-start.73 = (f32[8,3072]{1,0:T(8,128)S(1)}, f32[8,3072]{1,0:T(8,128)}, u32[]{:S(2)}, u32[]{:S(2)}) collective-permute-start(f32[8,3072]{1,0:T(8,128)S(1)} %copy-done.8), channel_id=1, source_target_pairs={{0,6},{1,7},{2,8},{3,9},{4,10},{5,11},{6,12},{7,13},{8,14},{9,15},... | collective-permute-start | bytes 294920
  (260 other events, 11204.0 us)
Sparse Core Ops, SparseCore 0:
  10.3 205.0 all-gather.11
  217.7 194.5 all-gather.13
  414.6 252.7 all-gather.15
  669.0 198.2 all-gather.17
  888.8 654.2 reduce-scatter.9
where the time goes:
time: 2030 us; the launch traced here: 2010 us
  blocking collectives  865 us (43%)
  waiting for transfers between devices  579 us (29%)
  starting transfers between devices  284 us (14%)
  local copies, waits for them, and re-layouts  153 us (8%)
  matrix products  85.7 us (4%)
  other arithmetic  24 us (1%)
    unnamed x3, blocking collectives  512 us
    ppermute x46, waiting for transfers between devices, from_behind(): return lax.ppermute(block, axis, route)  345 us
    unnamed x96, starting transfers between devices  267 us
    all_gather x1, waiting for transfers between devices, fetch_layer(): lax.all_gather(w_proj[layer_idx], ('dp', 'ctx'), axis=0, tiled=True)  193 us
    all_gather x1, blocking collectives, fetch_layer(): lax.all_gather(biases[layer_idx], ('dp', 'ctx'), axis=1, tiled=True)  181 us
    all_gather x1, blocking collectives, fetch_layer(): lax.all_gather(gains[layer_idx], ('dp', 'ctx'), axis=1, tiled=True)  172 us
    unnamed x293, local copies, waits for them, and re-layouts  129 us
  transfers between devices with their start and end apart: 147, of which 35 were waited for; matrix products, arithmetic and copies ran while one was open for 30% of the time, Pallas kernels for 0%

commit v1 on v0

v1 whole, which is shorter than its diff:
```python
import functools

import jax
import jax.numpy as jnp
import numpy as np
from jax import lax
from jax.experimental import pallas as pl
from jax.experimental.pallas import tpu as pltpu
from jax.sharding import PartitionSpec as P

BF = jnp.bfloat16
F32 = jnp.float32
MESH = pl.DeviceIdType.MESH
VMEM = pltpu.VMEM
ALL = slice(None)
AXES = ("x", "y", "z")
GATHER_ORDER = (("x", "y", "z"), ("y", "z", "x"), ("z", "x", "y"))
SHAPE_Q = (4, 12, 2, 4, 2, 48, 128)
SHAPE_P = (6, 2, 4, 2, 4, 48, 128)
SHAPE_V = (2, 4, 2, 4, 2, 16, 128)


def place():
    dp = lax.axis_index("dp")
    ctx = lax.axis_index("ctx")
    at = {
        "x": lax.rem(lax.div(ctx, 2), 4),
        "y": lax.rem(dp, 4),
        "z": lax.div(ctx, 8) * 2 + lax.div(dp, 4),
    }
    return at, lax.rem(ctx, 2)


def device(at, core):
    return {
        "dp": lax.rem(at["z"], 2) * 4 + at["y"],
        "ctx": lax.div(at["z"], 2) * 8 + at["x"] * 2 + core,
    }


def beside(at, axis, distance):
    moved = dict(at)
    moved[axis] = lax.rem(at[axis] + (distance + 4), 4)
    return moved


def split_z(z):
    if isinstance(z, tuple):
        return pl.ds(z[1], 1), ALL
    if isinstance(z, slice):
        return ALL, ALL
    return lax.rem(z, 2), lax.div(z, 2)


def line(value):
    return pl.ds(2 * value[1], 2) if isinstance(value, tuple) else value


def views(refs, part, sel, core, cut=None):
    ref_q, ref_p, ref_v = refs
    x, y = line(sel["x"]), line(sel["y"])
    zl, zh = split_z(sel["z"])
    first, count = (0, 3) if cut is None else ((0, 2), (2, 1))[cut]
    if part < 2:
        start = first + 3 * part + (0 if core is None else 6 * core)
        return [ref_q.at[x, pl.ds(start, count), zl, y, zh]]
    start = first + (0 if core is None else 3 * core)
    found = [ref_p.at[pl.ds(start, count), zl, y, zh, x]]
    if cut != 1:
        found.append(ref_v.at[zl, y, zh, x] if core is None else ref_v.at[zl, y, zh, x, core])
    return found


def greet(targets):
    barrier = pltpu.get_barrier_semaphore()
    for target in targets:
        pl.semaphore_signal(barrier, inc=1, device_id=target, device_id_type=MESH)
    pl.semaphore_wait(barrier, len(targets))


class Mail:
    def __init__(self, send_sem, recv_sem):
        self.send_sem, self.recv_sem, self.used, self.sent = send_sem, recv_sem, 0, []

    def send(self, sources, targets, device_id):
        keys = []
        for source, target in zip(sources, targets):
            copy = pltpu.make_async_remote_copy(
                src_ref=source,
                dst_ref=target,
                send_sem=self.send_sem.at[self.used],
                recv_sem=self.recv_sem.at[self.used],
                device_id=device_id,
                device_id_type=MESH,
            )
            copy.start()
            self.sent.append(copy)
            keys.append(self.used)
            self.used += 1
        return keys

    def receive(self, keys, arrivals, device_id):
        for key, arrival in zip(keys, arrivals):
            pltpu.make_async_remote_copy(
                src_ref=arrival,
                dst_ref=arrival,
                send_sem=self.send_sem.at[key],
                recv_sem=self.recv_sem.at[key],
                device_id=device_id,
                device_id_type=MESH,
            ).wait_recv()

    def finish(self):
        for copy in self.sent:
            copy.wait_send()


def group_and_neighbours(at, core):
    found = []
    spot = at["x"] * 2 + core
    for step in range(1, 8):
        other = lax.rem(spot + step, 8)
        found.append(device({**at, "x": lax.div(other, 2)}, lax.rem(other, 2)))
    for axis in ("y", "z"):
        for distance in (-1, 1):
            found.append(device(beside(at, axis, distance), core))
    return found


def gather_kernel(
    wq, wp, wv, place_q, place_p, all_q, all_p, all_v, in_q, in_p, own_q, own_p, send_sem, recv_sem, local_sem
):
    at, core = place()
    greet(group_and_neighbours(at, core))
    mail = Mail(send_sem, recv_sem)
    spot = at["x"] * 2 + core
    twin = device(at, 1 - core)

    waits = []
    for step in range(1, 8):
        other = lax.rem(spot + step, 8)
        source = lax.rem(spot + 8 - step, 8)
        target = device({**at, "x": lax.div(other, 2)}, lax.rem(other, 2))
        waits.append((mail.send([wq.at[other]], [in_q.at[spot]], target), [in_q.at[source]], target))
    waits.append((mail.send([wp.at[1 - core]], [in_p.at[core]], twin), [in_p.at[1 - core]], twin))
    in_q[spot] = wq[spot]
    in_p[core] = wp[core]
    for wait in waits:
        mail.receive(*wait)
    rows = jnp.dot(place_q[...], in_q[...].reshape(128, 768), preferred_element_type=F32).astype(BF)
    for tile in range(6):
        own_q[tile] = rows[:, 128 * tile : 128 * tile + 128]
    rows = jnp.dot(place_p[...], in_p[...].reshape(64, 384), preferred_element_type=F32).astype(BF)
    for tile in range(3):
        own_p[tile] = rows[:, 128 * tile : 128 * tile + 128]

    whole = (all_q, all_p, all_v)
    own = ([own_q.at[pl.ds(0, 3)]], [own_q.at[pl.ds(3, 3)]], [own_p, wv])
    local = []
    for part in range(3):
        for source, target in zip(own[part], views(whole, part, at, core)):
            copy = pltpu.make_async_copy(source, target, local_sem.at[len(local)])
            copy.start()
            local.append(copy)

    twin_keys = []

    def to_twin(part, sel):
        mine = views(whole, part, sel, core)
        twin_keys.append((mail.send(mine, mine, twin), views(whole, part, sel, 1 - core), twin))

    for phase in range(3):
        started = []
        for part in range(3):
            order = GATHER_ORDER[part]
            axis = order[phase]
            sel = dict(at)
            for done in order[:phase]:
                sel[done] = ALL
            mine = views(whole, part, sel, core)
            source = own[part] if phase == 0 else mine
            keys = []
            for distance in (1, -1):
                target = device(beside(at, axis, distance), core)
                keys.append(mail.send(source, mine, target))
            started.append((sel, keys))
        if phase == 0:
            for copy in local:
                copy.wait()
        forwards = []
        for part in range(3):
            order = GATHER_ORDER[part]
            axis = order[phase]
            sel, keys = started[part]
            pending = []
            for half, distance, key in ((0, 1, keys[0]), (1, -1, keys[1])):
                target = device(beside(at, axis, distance), core)
                arrived = beside(sel, axis, -distance)
                mail.receive(key, views(whole, part, arrived, core), target)
                far = beside(sel, axis, 2)
                if phase == 0:
                    moving = views(whole, part, arrived, core, cut=half)
                    coming = views(whole, part, far, core, cut=half)
                else:
                    arrived = {**arrived, order[0]: ("half", half)}
                    far = {**far, order[0]: ("half", half)}
                    moving = views(whole, part, arrived, core)
                    coming = views(whole, part, far, core)
                pending.append((mail.send(moving, moving, target), coming, target))
            if phase > 0:
                to_twin(part, beside(sel, axis, 1))
                to_twin(part, beside(sel, axis, -1))
            forwards.append(pending)
        for part in range(3):
            axis = GATHER_ORDER[part][phase]
            sel, _ = started[part]
            for wait in forwards[part]:
                mail.receive(*wait)
            to_twin(part, {**sel, axis: ALL} if phase == 0 else beside(sel, axis, 2))
    for wait in twin_keys:
        mail.receive(*wait)
    mail.finish()


def place_rows(groups, rows, padded):
    found = np.zeros((groups * rows, groups * padded), np.float32)
    for group in range(groups):
        for row in range(rows):
            found[group * rows + row, group * padded + row] = 1
    return found


def gather_weights(w_qkv, w_out, w_fc, w_proj, gains, biases, fc_bias):
    joint = jnp.concatenate([w_qkv[0], w_out[0], w_fc[0]], axis=1).reshape(6, 8, 768)
    wq = jnp.pad(jnp.transpose(joint, (1, 0, 2)), ((0, 0), (0, 10), (0, 0)))
    wp = jnp.pad(jnp.transpose(w_proj[0].reshape(24, 2, 384), (1, 0, 2)), ((0, 0), (0, 8), (0, 0)))
    small = jnp.pad(jnp.concatenate([gains[0], biases[0]], axis=0), ((0, 0), (0, 122)))
    wv = jnp.concatenate([small, jnp.pad(fc_bias, ((0, 0), (0, 104))), jnp.zeros((7, 128), BF)], axis=0)
    spaces = [pl.BlockSpec(memory_space=VMEM)] * 5
    return pl.pallas_call(
        gather_kernel,
        out_shape=[jax.ShapeDtypeStruct(shape, BF) for shape in (SHAPE_Q, SHAPE_P, SHAPE_V)],
        in_specs=spaces,
        out_specs=[pl.BlockSpec(memory_space=pl.ANY)] * 3,
        scratch_shapes=[
            VMEM((8, 16, 768), BF),
            VMEM((2, 32, 384), BF),
            VMEM((6, 48, 128), BF),
            VMEM((3, 48, 128), BF),
            pltpu.SemaphoreType.DMA((96,)),
            pltpu.SemaphoreType.DMA((96,)),
            pltpu.SemaphoreType.DMA((4,)),
        ],
        compiler_params=pltpu.CompilerParams(
            collective_id=0, has_side_effects=True, vmem_limit_bytes=16 * 1024 * 1024
        ),
        name="gather_weights",
    )(
        wq,
        wp,
        wv,
        jnp.asarray(place_rows(8, 6, 16), BF),
        jnp.asarray(place_rows(2, 24, 32), BF),
    )
REDUCE_ORDER = tuple(order[::-1] for order in GATHER_ORDER)


def added(target, *terms):
    if len(target.shape) == 2:
        total = target[...].astype(F32)
        for term in terms:
            total = total + term[...].astype(F32)
        target[...] = total.astype(BF)
        return
    count = target.shape[0]

    def step(i, carry):
        total = target[i].astype(F32)
        for term in terms:
            total = total + term[i].astype(F32)
        target[i] = total.astype(BF)
        return carry

    lax.fori_loop(0, count, step, 0)


def block_shapes(part, gone, cut, half_axis):
    extent = {axis: 1 if axis in gone else 4 for axis in AXES}
    if half_axis is not None:
        extent[half_axis] = 2
    count = 3 if cut is None else (2, 1)[cut]
    if extent["z"] == 1:
        z_dims = ()
    else:
        z_dims = (extent["z"] // 2, 2)
    lead = lambda name: () if extent[name] == 1 else (extent[name],)
    zl = z_dims[:1]
    zh = z_dims[1:]
    if part < 2:
        return [lead("x") + (count,) + zl + lead("y") + zh + (48, 128)]
    found = [(count,) + zl + lead("y") + zh + lead("x") + (48, 128)]
    if cut != 1:
        found.append(zl + lead("y") + zh + lead("x") + (16, 128))
    return found


def reduce_buffers():
    found = []
    for phase in range(3):
        for part in range(3):
            order = REDUCE_ORDER[part]
            gone = order[: phase + 1]
            half_axis = order[2] if phase < 2 else None
            for half in range(2):
                cut = half if phase == 2 else None
                shapes = block_shapes(part, gone, cut, half_axis)
                for _ in range(3):
                    found.append(shapes)
    return found


def reduce_kernel(*refs):
    shapes = reduce_buffers()
    grads = refs[:3]
    spread_q, spread_p = refs[3:5]
    out_q, out_p, out_v = refs[5:8]
    acc = refs[8:11]
    flat_at = 11
    buffers = []
    for group in shapes:
        buffers.append(refs[flat_at : flat_at + len(group)])
        flat_at += len(group)
    last_q, last_p, in_q, in_p, send_sem, recv_sem = refs[flat_at:]

    at, core = place()
    greet(group_and_neighbours(at, core))
    mail = Mail(send_sem, recv_sem)
    spot = at["x"] * 2 + core
    twin = device(at, 1 - core)
    every = {axis: ALL for axis in AXES}

    waits = []
    for part in range(3):
        arrivals = views(acc, part, every, None)
        waits.append((mail.send(views(grads, part, every, 1 - core), arrivals, twin), arrivals, twin))

    def halves(part, phase, sel, half):
        if phase == 2:
            return views(acc, part, sel, None, cut=half)
        return views(acc, part, {**sel, REDUCE_ORDER[part][2]: ("half", half)}, None)

    for phase in range(3):
        first = []
        for part in range(3):
            if phase == 0:
                mail.receive(*waits[part])
                for total, term in zip(views(acc, part, every, None), views(grads, part, every, core)):
                    added(total, term)
            axis = REDUCE_ORDER[part][phase]
            sel = dict(at)
            for later in REDUCE_ORDER[part][phase + 1 :]:
                sel[later] = ALL
            base = (phase * 3 + part) * 6
            landing = [buffers[base + 3 * half : base + 3 * half + 3] for half in range(2)]
            far, up, down = beside(sel, axis, 2), beside(sel, axis, 1), beside(sel, axis, -1)
            plus = device(beside(at, axis, 1), core)
            minus = device(beside(at, axis, -1), core)
            far_keys = [
                mail.send(halves(part, phase, far, 0), landing[0][0], plus),
                mail.send(halves(part, phase, far, 1), landing[1][0], minus),
            ]
            up_keys = mail.send(halves(part, phase, up, 1), landing[1][1], plus)
            down_keys = mail.send(halves(part, phase, down, 0), landing[0][2], minus)
            first.append((sel, landing, up, down, plus, minus, far_keys, up_keys, down_keys))
        second = []
        for part in range(3):
            sel, landing, up, down, plus, minus, far_keys, _, _ = first[part]
            mail.receive(far_keys[0], landing[0][0], plus)
            for total, term in zip(halves(part, phase, up, 0), landing[0][0]):
                added(total, term)
            plus_keys = mail.send(halves(part, phase, up, 0), landing[0][1], plus)
            mail.receive(far_keys[1], landing[1][0], minus)
            for total, term in zip(halves(part, phase, down, 1), landing[1][0]):
                added(total, term)
            minus_keys = mail.send(halves(part, phase, down, 1), landing[1][2], minus)
            second.append((plus_keys, minus_keys))
        for part in range(3):
            sel, landing, up, down, plus, minus, _, up_keys, down_keys = first[part]
            plus_keys, minus_keys = second[part]
            mail.receive(up_keys, landing[1][1], plus)
            mail.receive(minus_keys, landing[1][2], minus)
            for total, one, two in zip(halves(part, phase, sel, 1), landing[1][1], landing[1][2]):
                added(total, one, two)
            mail.receive(plus_keys, landing[0][1], plus)
            mail.receive(down_keys, landing[0][2], minus)
            for total, one, two in zip(halves(part, phase, sel, 0), landing[0][1], landing[0][2]):
                added(total, one, two)

    mine = [views(acc, part, at, None) for part in range(3)]
    rows = jnp.concatenate([mine[tile // 3][0][tile % 3] for tile in range(6)], axis=1)
    last_q[...] = jnp.dot(spread_q[...], rows, preferred_element_type=F32).astype(BF).reshape(8, 16, 768)
    rows = jnp.concatenate([mine[2][0][tile] for tile in range(3)], axis=1)
    last_p[...] = jnp.dot(spread_p[...], rows, preferred_element_type=F32).astype(BF).reshape(2, 32, 384)
    waits = []
    for step in range(1, 8):
        other = lax.rem(spot + step, 8)
        source = lax.rem(spot + 8 - step, 8)
        target = device({**at, "x": lax.div(other, 2)}, lax.rem(other, 2))
        waits.append((mail.send([last_q.at[other]], [in_q.at[spot]], target), [in_q.at[source]], target))
    waits.append((mail.send([last_p.at[1 - core]], [in_p.at[core]], twin), [in_p.at[1 - core]], twin))
    in_q[spot] = last_q[spot]
    in_p[core] = last_p[core]
    out_v[...] = mine[2][1][...].astype(F32)
    for wait in waits:
        mail.receive(*wait)
    for group in range(8):
        out_q[:, 768 * group : 768 * group + 768] = in_q[group].astype(F32)[:8]
    for half in range(2):
        out_p[:, 384 * half : 384 * half + 384] = in_p[half].astype(F32)[:24]
    mail.finish()


def reduce_grads(grad_q, grad_p, grad_v):
    scratch = [VMEM((4, 6, 2, 4, 2, 48, 128), BF), VMEM((3, 2, 4, 2, 4, 48, 128), BF), VMEM((2, 4, 2, 4, 16, 128), BF)]
    for group in reduce_buffers():
        scratch += [VMEM(shape, BF) for shape in group]
    scratch += [
        VMEM((8, 16, 768), BF),
        VMEM((2, 32, 384), BF),
        VMEM((8, 16, 768), BF),
        VMEM((2, 32, 384), BF),
        pltpu.SemaphoreType.DMA((100,)),
        pltpu.SemaphoreType.DMA((100,)),
    ]
    return pl.pallas_call(
        reduce_kernel,
        out_shape=[
            jax.ShapeDtypeStruct((8, 6144), F32),
            jax.ShapeDtypeStruct((24, 768), F32),
            jax.ShapeDtypeStruct((16, 128), F32),
        ],
        in_specs=[pl.BlockSpec(memory_space=VMEM)] * 5,
        out_specs=[pl.BlockSpec(memory_space=VMEM)] * 3,
        scratch_shapes=scratch,
        compiler_params=pltpu.CompilerParams(
            collective_id=1, has_side_effects=True, vmem_limit_bytes=56 * 1024 * 1024
        ),
        name="reduce_grads",
    )(
        grad_q,
        grad_p,
        grad_v,
        jnp.asarray(place_rows(8, 6, 16).T, BF),
        jnp.asarray(place_rows(2, 24, 32).T, BF),
    )
HEADS = 12
WIDTH = 768
HIDDEN = 3072
NORM_EPS = 1e-05
MASKED = -1e30
MEGA = 1024 * 1024


def dot(left, right):
    return jnp.dot(left, right, preferred_element_type=F32)


def dot_right_t(left, right):
    return lax.dot_general(left, right, (((1,), (1,)), ((), ())), preferred_element_type=F32)


def dot_left_t(left, right):
    return lax.dot_general(left, right, (((0,), (0,)), ((), ())), preferred_element_type=F32)


def mean_last(values):
    return jnp.mean(values, axis=-1, keepdims=True)


def normalize(values):
    center = values - mean_last(values)
    factor = lax.rsqrt(mean_last(center * center) + NORM_EPS)
    return center * factor, factor


def norm_back(d_norm, xhat, factor, gain):
    e = d_norm * gain
    return factor * (e - mean_last(e) - xhat * mean_last(e * xhat))


def owner_mask(rows, extra, columns, each):
    shape = (128, extra, columns) if extra else (128, columns)
    owner = lax.broadcasted_iota(jnp.int32, shape, 0) * each
    column = lax.broadcasted_iota(jnp.int32, shape, len(shape) - 1)
    return (column >= owner) & (column < owner + each)


def spread_matrix(columns, each):
    found = np.zeros((128, columns), np.float32)
    found[np.arange(columns) % each, np.arange(columns)] = 1
    return found


def fetch(source, target, sem):
    copy = pltpu.make_async_copy(source, target, sem)
    copy.start()
    return copy


def query_kernel(x, small, spread, spread_fc, all_q, normed, qkv_t, vectors, hidden_bias, w, sem):
    coming = fetch(all_q.at[pl.ds(0, 18)], w, sem)
    small_rows = small[...]
    wide = dot(small_rows, spread[...]).reshape(128, 16, WIDTH)
    found = jnp.sum(jnp.where(owner_mask(128, 16, WIDTH, 6), wide, 0.0), axis=0)
    vectors[...] = found
    tall = small_rows.astype(F32).reshape(128, 16, 128)
    pick = lax.broadcasted_iota(jnp.int32, (128, 16, 128), 1) == 8
    fc_rows = jnp.sum(jnp.where(pick, tall, 0.0), axis=1).astype(BF)
    wide = dot(fc_rows, spread_fc[...])
    hidden_bias[...] = jnp.sum(jnp.where(owner_mask(128, 0, HIDDEN, 24), wide, 0.0), axis=0, keepdims=True)
    xhat, _ = normalize(x[...])
    rows = (xhat * found[0:1] + found[2:3]).astype(BF)
    normed[...] = rows
    coming.wait()
    for pair in range(9):
        kind, first = pair // 3, (pair % 3) * 256
        out = dot(rows, jnp.concatenate([w[2 * pair], w[2 * pair + 1]], axis=1))
        if kind != 1:
            out = out + found[3 + kind // 2 : 4 + kind // 2, first : first + 256]
        out = out.astype(BF).astype(F32).T.astype(BF)
        for head in range(4):
            qkv_t[first // 64 + head, 64 * kind : 64 * kind + 64, :] = out[64 * head : 64 * head + 64]


def local_call(kernel, name, ins, outs, scratch=(), limit=56, in_specs=None, flops=0):
    return pl.pallas_call(
        kernel,
        out_shape=[jax.ShapeDtypeStruct(shape, kind) for shape, kind in outs],
        in_specs=in_specs or [pl.BlockSpec(memory_space=VMEM)] * len(ins),
        out_specs=[pl.BlockSpec(memory_space=VMEM)] * len(outs),
        scratch_shapes=list(scratch),
        compiler_params=pltpu.CompilerParams(vmem_limit_bytes=limit * MEGA),
        name=name,
    )(*ins)


def ctx_peers(ctx):
    return [lax.rem(ctx + step, 16) for step in range(1, 16)]


def to_heads_kernel(block, out, send_sem, recv_sem, local_sem):
    ctx = lax.axis_index("ctx")
    greet([{"ctx": peer} for peer in ctx_peers(ctx)])
    span = lambda who: out.at[:, pl.ds(pl.multiple_of(who * 128, 128), 128)]
    for step in range(1, 16):
        peer = lax.rem(ctx + step, 16)

        @pl.when(peer < HEADS)
        def _():
            pltpu.make_async_remote_copy(
                block.at[peer], span(ctx), send_sem.at[step], recv_sem.at[step],
                device_id={"ctx": peer}, device_id_type=MESH,
            ).start()

    @pl.when(ctx < HEADS)
    def _():
        copy = pltpu.make_async_copy(block.at[ctx], span(ctx), local_sem)
        copy.start()
        for step in range(1, 16):
            source = lax.rem(ctx + 16 - step, 16)
            pltpu.make_async_remote_copy(
                span(source), span(source), send_sem.at[step], recv_sem.at[step],
                device_id={"ctx": source}, device_id_type=MESH,
            ).wait_recv()
        copy.wait()

    for step in range(1, 16):
        peer = lax.rem(ctx + step, 16)

        @pl.when(peer < HEADS)
        def _():
            pltpu.make_async_remote_copy(
                block.at[peer], span(ctx), send_sem.at[step], recv_sem.at[step],
                device_id={"ctx": peer}, device_id_type=MESH,
            ).wait_send()


def from_heads_kernel(blocks, out, send_sem, recv_sem, local_sem):
    ctx = lax.axis_index("ctx")
    greet([{"ctx": peer} for peer in ctx_peers(ctx)])

    @pl.when(ctx < HEADS)
    def _():
        for step in range(1, 16):
            peer = lax.rem(ctx + step, 16)
            pltpu.make_async_remote_copy(
                blocks.at[peer], out.at[ctx], send_sem.at[step], recv_sem.at[step],
                device_id={"ctx": peer}, device_id_type=MESH,
            ).start()
        copy = pltpu.make_async_copy(blocks.at[ctx], out.at[ctx], local_sem)
        copy.start()
        copy.wait()

    for step in range(1, 16):
        source = lax.rem(ctx + 16 - step, 16)

        @pl.when(source < HEADS)
        def _():
            pltpu.make_async_remote_copy(
                out.at[source], out.at[source], send_sem.at[step], recv_sem.at[step],
                device_id={"ctx": source}, device_id_type=MESH,
            ).wait_recv()

    @pl.when(ctx < HEADS)
    def _():
        for step in range(1, 16):
            peer = lax.rem(ctx + step, 16)
            pltpu.make_async_remote_copy(
                blocks.at[peer], out.at[ctx], send_sem.at[step], recv_sem.at[step],
                device_id={"ctx": peer}, device_id_type=MESH,
            ).wait_send()


def exchange(kernel, name, collective_id, block, out_shape):
    return pl.pallas_call(
        kernel,
        out_shape=jax.ShapeDtypeStruct(out_shape, BF),
        in_specs=[pl.BlockSpec(memory_space=VMEM)],
        out_specs=pl.BlockSpec(memory_space=VMEM),
        scratch_shapes=[
            pltpu.SemaphoreType.DMA((16,)),
            pltpu.SemaphoreType.DMA((16,)),
            pltpu.SemaphoreType.DMA,
        ],
        compiler_params=pltpu.CompilerParams(
            collective_id=collective_id, has_side_effects=True, vmem_limit_bytes=16 * MEGA
        ),
        name=name,
    )(block)


def low_half(shape):
    return lax.broadcasted_iota(jnp.int32, shape, 1) < 64


def swap_halves(tile):
    return pltpu.roll(tile, 64, 1)


def position_tile(block, tile):
    if tile < 8:
        low, high = block(2 * tile), swap_halves(block(2 * tile + 1))
    else:
        low, high = swap_halves(block(31 - 2 * tile)), block(30 - 2 * tile)
    return jnp.where(low_half(low.shape), low, high)


def position_block(tile, block):
    early, late = tile(block // 2), tile((31 - block) // 2)
    if block % 2 == 0:
        return jnp.where(low_half(early.shape), early, late)
    return swap_halves(jnp.where(low_half(early.shape), late, early))


TILE = 256


def causal(scores, first):
    rows, columns = scores.shape
    key = lax.broadcasted_iota(jnp.int32, (rows, columns), 0)
    query = lax.broadcasted_iota(jnp.int32, (rows, columns), 1) + first
    return jnp.where(key <= query, scores, MASKED)


def attend_kernel(landed, ordered, natural, out_t, log_total, blocks):
    for tile in range(16):
        found = position_tile(lambda b: landed[:, 128 * b : 128 * b + 128].astype(F32), tile)
        found = jnp.concatenate([found[0:64] * 0.125, found[64:192]], axis=0)
        span = slice(128 * tile, 128 * tile + 128)
        ordered[:, span] = found.astype(BF)
        natural[span, :] = found.T.astype(BF)
    for step in range(2048 // TILE):
        first = TILE * step
        count = first + TILE
        span = slice(first, count)
        scores = dot(natural[0:count, 64:128], ordered[0:64, span])
        scores = causal(scores, first)
        best = jnp.max(scores, axis=0, keepdims=True)
        probs = jnp.exp(scores - best)
        total = jnp.sum(probs, axis=0, keepdims=True)
        out_t[:, span] = dot(ordered[128:192, 0:count], probs.astype(BF)) / total
        log_total[0:1, span] = best + jnp.log(total)
    for block in range(16):
        blocks[block] = position_block(lambda t: out_t[:, 128 * t : 128 * t + 128], block).astype(BF)


def attend_back_kernel(ordered, natural, out_t, log_total, landed, blocks, d_out, d_out_nat, d_t, d_keys, d_values):
    for tile in range(16):
        found = position_tile(lambda b: landed[:, 128 * b : 128 * b + 128].astype(F32), tile)
        span = slice(128 * tile, 128 * tile + 128)
        d_out[:, span] = found
        d_out_nat[span, :] = found.T.astype(BF)
    d_keys[...] = jnp.zeros_like(d_keys)
    d_values[...] = jnp.zeros_like(d_values)
    for step in range(2048 // TILE):
        first = TILE * step
        count = first + TILE
        span = slice(first, count)
        scores = causal(dot(natural[0:count, 64:128], ordered[0:64, span]), first)
        probs = jnp.exp(scores - log_total[0:1, span])
        d_here = d_out[:, span]
        delta = jnp.sum(d_here * out_t[:, span], axis=0, keepdims=True)
        d_probs = dot(natural[0:count, 128:192], d_here.astype(BF))
        d_scores = (probs * (d_probs - delta)).astype(BF)
        d_t[0:64, span] = dot(ordered[64:128, 0:count], d_scores) * 0.125
        d_keys[0:count, :] += dot(d_scores, natural[span, 0:64])
        d_values[0:count, :] += dot(probs.astype(BF), d_out_nat[span, :])
    for tile in range(16):
        span = slice(128 * tile, 128 * tile + 128)
        d_t[64:128, span] = d_keys[span, :].T
        d_t[128:192, span] = d_values[span, :].T
    for block in range(16):
        blocks[block] = position_block(lambda t: d_t[:, 128 * t : 128 * t + 128], block).astype(BF)


CHUNK = 4


def middle_kernel(
    x, cotangent, att_t, vectors, hidden_bias, all_q, all_p,
    final, d_middle, d_att_t, grad_q, grad_p, grad_vectors, grad_hidden,
    total, d_norm_two, w_rest, w_proj, sem_out, sem_fc, sem_proj,
):
    coming_out = fetch(all_q.at[pl.ds(18, 6)], w_rest.at[pl.ds(0, 6)], sem_out)
    coming_fc = fetch(all_q.at[pl.ds(24, 24)], w_rest.at[pl.ds(6, 24)], sem_fc)
    coming_proj = fetch(all_p, w_proj, sem_proj)
    wide = lambda ref, first, count: jnp.concatenate([ref[first + i] for i in range(count)], axis=1)
    rows_t = att_t[...]
    coming_out.wait()
    mat_out = wide(w_rest, 0, 6)
    attended = rows_t.astype(F32).T.astype(BF)
    middle = x[...] + dot(attended, mat_out) + vectors[5:6]
    xhat, factor = normalize(middle)
    normed = (xhat * vectors[1:2] + vectors[6:7]).astype(BF)
    normed_t = normed.astype(F32).T.astype(BF)
    gradient = cotangent[...]
    d_two = gradient.astype(BF)
    total[...] = jnp.zeros_like(total)
    d_norm_two[...] = jnp.zeros_like(d_norm_two)

    coming_fc.wait()
    coming_proj.wait()

    def chunk(i, carry):
        span = pl.ds(pl.multiple_of(i * CHUNK * 128, CHUNK * 128), CHUNK * 128)
        mat_fc = jnp.concatenate([w_rest[6 + i * CHUNK + j] for j in range(CHUNK)], axis=1)
        mat_proj = jnp.concatenate([w_proj[j, span] for j in range(6)], axis=1)
        pre = dot(normed, mat_fc) + hidden_bias[:, span]
        root = 0.7978845608028654
        inner = jnp.tanh(root * (pre + 0.044715 * (pre * pre * pre)))
        activated = (0.5 * pre * (1.0 + inner)).astype(BF)
        slope = 0.5 * (1.0 + inner) + 0.5 * pre * (1.0 - inner * inner) * (
            root * (1.0 + 3 * 0.044715 * (pre * pre))
        )
        total[...] += dot(activated, mat_proj)
        d_pre = (dot_right_t(d_two, mat_proj) * slope).astype(BF)
        grad_hidden[:, span] = jnp.sum(d_pre.astype(F32), axis=0, keepdims=True)
        d_norm_two[...] += dot_right_t(d_pre, mat_fc)
        grad_fc = dot(normed_t, d_pre).astype(BF)
        for j in range(CHUNK):
            grad_q[6 + i * CHUNK + j] = grad_fc[:, 128 * j : 128 * j + 128]
        grad_proj = dot_left_t(activated, d_two).astype(BF)
        for j in range(6):
            grad_p[j, span] = grad_proj[:, 128 * j : 128 * j + 128]
        return carry

    lax.fori_loop(0, 24 // CHUNK, chunk, 0)
    final[...] = middle + total[...] + vectors[7:8]
    d_norm = d_norm_two[...]
    d_mid = gradient + norm_back(d_norm, xhat, factor, vectors[1:2])
    d_middle[...] = d_mid
    d_one = d_mid.astype(BF)
    d_att_t[...] = dot_right_t(mat_out, d_one).astype(BF)
    grad_out = dot(rows_t, d_one).astype(BF)
    for j in range(6):
        grad_q[j] = grad_out[:, 128 * j : 128 * j + 128]
    sums = lambda values: jnp.sum(values, axis=0, keepdims=True)
    grad_vectors[...] = jnp.zeros_like(grad_vectors)
    grad_vectors[1:2] = sums(d_norm * xhat)
    grad_vectors[5:6] = sums(d_one.astype(F32))
    grad_vectors[6:7] = sums(d_norm)
    grad_vectors[7:8] = sums(d_two.astype(F32))


def last_kernel(
    x, normed, d_middle, d_qkv_t, vectors, grad_vectors, grad_hidden, spread, spread_fc, all_q,
    input_grad, grad_q, grad_small, d_qkv, w, sem,
):
    coming = fetch(all_q.at[pl.ds(0, 18)], w, sem)
    for head in range(HEADS):
        rows = d_qkv_t[head].astype(F32).T.astype(BF)
        for kind in range(3):
            first = WIDTH * kind + 64 * head
            d_qkv[:, first : first + 64] = rows[:, 64 * kind : 64 * kind + 64]
    normed_t = normed[...].astype(F32).T.astype(BF)
    d_norm = jnp.zeros((128, WIDTH), F32)
    coming.wait()
    for pair in range(9):
        part = d_qkv[:, 256 * pair : 256 * pair + 256]
        out = dot(normed_t, part).astype(BF)
        grad_q[2 * pair] = out[:, :128]
        grad_q[2 * pair + 1] = out[:, 128:]
        d_norm = d_norm + dot_right_t(part, jnp.concatenate([w[2 * pair], w[2 * pair + 1]], axis=1))
    xhat, factor = normalize(x[...])
    input_grad[...] = d_middle[...] + norm_back(d_norm, xhat, factor, vectors[0:1])
    sums = lambda values: jnp.sum(values, axis=0, keepdims=True)
    kinds = lambda kind: sums(d_qkv[:, WIDTH * kind : WIDTH * kind + WIDTH].astype(F32))
    row = lax.broadcasted_iota(jnp.int32, (16, WIDTH), 0)
    found = grad_vectors[...]
    for at, value in ((0, sums(d_norm * xhat)), (2, sums(d_norm)), (3, kinds(0)), (4, kinds(2))):
        found = jnp.where(row == at, value, found)
    wide = jnp.broadcast_to(found[None], (128, 16, WIDTH))
    wide = jnp.where(owner_mask(128, 16, WIDTH, 6), wide, 0.0).astype(BF).reshape(2048, WIDTH)
    small = dot_right_t(wide, spread[...]).reshape(128, 16, 128)
    wide = jnp.where(owner_mask(128, 0, HIDDEN, 24), jnp.broadcast_to(grad_hidden[...], (128, HIDDEN)), 0.0)
    hidden = dot_right_t(wide.astype(BF), spread_fc[...])
    place_at = lax.broadcasted_iota(jnp.int32, (128, 16, 128), 1) == 8
    small = jnp.where(place_at, hidden[:, None, :], small)
    grad_small[...] = small.astype(BF)


def local(tokens, cotangent, w_qkv, w_out, w_fc, w_proj, gains, biases, fc_bias):
    x = tokens[0]
    all_q, all_p, all_v = gather_weights(w_qkv, w_out, w_fc, w_proj, gains, biases, fc_bias)
    all_q = all_q.reshape(48, WIDTH, 128)
    all_p = all_p.reshape(6, HIDDEN, 128)
    small = all_v.reshape(2048, 128)
    spread = jnp.asarray(spread_matrix(WIDTH, 6), BF)
    spread_fc = jnp.asarray(spread_matrix(HIDDEN, 24), BF)
    whole = pl.BlockSpec(memory_space=VMEM)
    stay = pl.BlockSpec(memory_space=pl.ANY)
    first_w = [VMEM((18, WIDTH, 128), BF), pltpu.SemaphoreType.DMA]
    normed, qkv_t, vectors, hidden_bias = local_call(
        query_kernel,
        "query_keys_values",
        (x, small, spread, spread_fc, all_q),
        (((128, WIDTH), BF), ((HEADS, 192, 128), BF), ((16, WIDTH), F32), ((1, HIDDEN), F32)),
        scratch=first_w,
        in_specs=[whole] * 4 + [stay],
    )
    landed = exchange(to_heads_kernel, "rows_to_heads", 2, qkv_t, (192, 2048))
    ordered, natural, out_t, log_total, blocks = local_call(
        attend_kernel,
        "attend",
        (landed,),
        (((192, 2048), BF), ((2048, 192), BF), ((64, 2048), F32), ((8, 2048), F32), ((16, 64, 128), BF)),
    )
    att_t = exchange(from_heads_kernel, "heads_to_rows", 3, blocks, (HEADS, 64, 128)).reshape(WIDTH, 128)
    final, d_middle, d_att_t, grad_rest, grad_p, grad_vectors, grad_hidden = local_call(
        middle_kernel,
        "feed_forward_both_ways",
        (x, cotangent[0], att_t, vectors, hidden_bias, all_q, all_p),
        (
            ((128, WIDTH), F32),
            ((128, WIDTH), F32),
            ((WIDTH, 128), BF),
            ((30, WIDTH, 128), BF),
            ((6, HIDDEN, 128), BF),
            ((16, WIDTH), F32),
            ((1, HIDDEN), F32),
        ),
        scratch=[
            VMEM((128, WIDTH), F32),
            VMEM((128, WIDTH), F32),
            VMEM((30, WIDTH, 128), BF),
            VMEM((6, HIDDEN, 128), BF),
            pltpu.SemaphoreType.DMA,
            pltpu.SemaphoreType.DMA,
            pltpu.SemaphoreType.DMA,
        ],
        in_specs=[whole] * 5 + [stay, stay],
    )
    landed = exchange(to_heads_kernel, "gradient_to_heads", 4, d_att_t.reshape(HEADS, 64, 128), (64, 2048))
    (blocks,) = local_call(
        attend_back_kernel,
        "attend_back",
        (ordered, natural, out_t, log_total, landed),
        (((16, 192, 128), BF),),
        scratch=[
            VMEM((64, 2048), F32),
            VMEM((2048, 64), BF),
            VMEM((192, 2048), F32),
            VMEM((2048, 64), F32),
            VMEM((2048, 64), F32),
        ],
    )
    d_qkv_t = exchange(from_heads_kernel, "gradient_to_rows", 5, blocks, (HEADS, 192, 128))
    input_grad, grad_first, grad_small = local_call(
        last_kernel,
        "input_gradient",
        (x, normed, d_middle, d_qkv_t, vectors, grad_vectors, grad_hidden, spread, spread_fc, all_q),
        (((128, WIDTH), F32), ((18, WIDTH, 128), BF), ((128, 16, 128), BF)),
        scratch=[VMEM((128, 3 * WIDTH), BF)] + first_w,
        in_specs=[whole] * 9 + [stay],
    )
    grad_q = jnp.concatenate([grad_first, grad_rest], axis=0).reshape(SHAPE_Q)
    joint, proj, small = reduce_grads(grad_q, grad_p.reshape(SHAPE_P), grad_small.reshape(SHAPE_V))
    joint = joint[:6]
    return (
        final[None],
        input_grad[None],
        joint[None, :, : 3 * WIDTH],
        joint[None, :, 3 * WIDTH : 4 * WIDTH],
        joint[None, :, 4 * WIDTH :],
        proj[None],
        small[None, 0:2, :6],
        small[None, 2:8, :6],
        small[8:9, :24],
    )


def solution(mesh):
    rows = P("dp", "ctx", None)
    weight = P(None, ("dp", "ctx"), None)
    vector = P(None, None, ("dp", "ctx"))
    tail = (weight,) * 4 + (vector, vector, P(None, ("dp", "ctx")))
    return jax.shard_map(
        local, mesh=mesh, in_specs=(rows, rows) + tail, out_specs=(rows, rows) + tail, check_vma=False
    )
```

time: 2030 us -> 256 us (0.13)
  blocking collectives: 865 us -> 0 us
  waiting for transfers between devices: 579 us -> 0 us
  starting transfers between devices: 284 us -> 0 us
  Pallas kernels: 0 us -> 219 us
  local copies, waits for them, and re-layouts: 153 us -> 25.8 us
  matrix products: 85.7 us -> 0 us
    unnamed x3 -> x0, blocking collectives: 512 us -> none
    all_gather x2 -> x0, blocking collectives: 353 us -> none  [the longest x1 181 us: fetch_layer(): lax.all_gather(biases[layer_idx], ('dp', 'ctx'), axis=1, tiled=True)]
    ppermute x46 -> x0, waiting for transfers between devices: 345 us -> none  [from_behind(): return lax.ppermute(block, axis, route)]
    unnamed x96 -> x0, starting transfers between devices: 267 us -> none
    all_gather x4 -> x0, waiting for transfers between devices: 233 us -> none  [the longest x1 193 us: fetch_layer(): lax.all_gather(w_proj[layer_idx], ('dp', 'ctx'), axis=0, tiled=True)]
    pallas_call x0 -> x11, Pallas kernels: none -> 219 us  [the longest x1 67.1 us: reduce_grads(): pl.pallas_call(reduce_kernel, out_shape=[jax.ShapeDtypeStruct((8, 6144),...]
    unnamed x293 -> x35, local copies, waits for them, and re-layouts: 129 us -> 19.3 us
    dot_general x123 -> x0, matrix products: 85.7 us -> none  [the longest x4 15.9 us: rows_product(): lax.dot_general(left, right, (((0,), (0,)), ((), ())), preferred_element_...]
  transfers between devices with their start and end apart: 147 -> 0, of which waited for: 35 -> 0; matrix products, arithmetic and copies ran while one was open for 30% -> 0% of each run, Pallas kernels for 0% -> 0%
where the time goes in v1:
time: 256 us; the launch traced here: 254 us
  Pallas kernels  219 us (86%)
  local copies, waits for them, and re-layouts  25.8 us (10%)
  other arithmetic  8.7 us (3%)
    pallas_call x1, Pallas kernels, reduce_grads(): pl.pallas_call(reduce_kernel, out_shape=[jax.ShapeDtypeStruct((8, 6144),...  67.1 us
    pallas_call x1, Pallas kernels, gather_weights(): pl.pallas_call(gather_kernel, out_shape=[jax.ShapeDtypeStruct(shape, BF)...  55.1 us
    pallas_call x5, Pallas kernels, local_call(): pl.pallas_call(kernel, out_shape=[jax.ShapeDtypeStruct(shape, kind) for s...  49.7 us
    pallas_call x4, Pallas kernels, exchange(): pl.pallas_call(kernel, out_shape=jax.ShapeDtypeStruct(out_shape, BF), in_...  47.3 us
    unnamed x35, local copies, waits for them, and re-layouts  19.3 us
    concatenate x1, other arithmetic, local(): grad_q = jnp.concatenate([grad_first, grad_rest], axis=0).reshape(SHAPE_Q)  6.44 us

profile of v1, /device:TPU:1, one launch (start us, length us, event | category | flops | bytes accessed | tf_op | source)
XLA Modules:
  0.0 254.4 jit_solution(18117201534421924161)
XLA Ops:
  5.2 55.1 %gather_weights.1 = (bf16[4,12,2,4,2,48,128]{6,5,4,3,2,1,0:T(8,128)(2,1)S(1)}, bf16[6,2,4,2,4,48,128]{6,5,4,3,2,1,0:T(8,128)(2,1)S(1)}, bf16[2,4,2,4,2,16,128]{6,5,4,3,2,1,0:T(8,128)(2,1)S(1)}) custom-call(bf16[8,16,768]{2,1,0:T(8,128)(2,1)S(1)} %pad.16.wq, bf16[2,32,384]{2,1,0:T(8,128)(2,1)S(1)} %pad.17.wp, bf16[16,128]{1,0:T(8,128)(2,1)S(1)} %fusion.3.wv, ...), custom_call_target="tpu_custom_call" | custom-call | tf_op jit(solution)/shard_map/gather_weights/pallas_call | solution.py:240
  60.4 3.7 %copy-done = bf16[4,12,2,4,2,48,128]{6,5,4,3,2,1,0:T(8,128)(2,1)} copy-done((bf16[4,12,2,4,2,48,128]{6,5,4,3,2,1,0:T(8,128)(2,1)}, bf16[4,12,2,4,2,48,128]{6,5,4,3,2,1,0:T(8,128)(2,1)S(1)}, u32[]{:S(2)}) %copy-start) | copy-done | bytes 9437208
  64.0 2.1 copy-done.1
  67.0 5.1 %query_keys_values.1 = (bf16[128,768]{1,0:T(8,128)(2,1)}, bf16[12,192,128]{2,1,0:T(8,128)(2,1)}, f32[16,768]{1,0:T(8,128)}, f32[1,3072]{1,0:T(1,128)}) custom-call(f32[128,768]{1,0:T(8,128)} %bitcast.45, bf16[2048,128]{1,0:T(8,128)(2,1)} %bitcast.39, bf16[128,768]{1,0:T(8,128)(2,1)} %constant.18.clone.spread, bf16[128,3072]{1,0:T(8,128)(2,1)} %constant.19.clone.spread_fc, ...), custom_call_target="tpu_custom_call" | custom-call | tf_op jit(solution)/shard_map/query_keys_values/pallas_call | solution.py:536
  72.1 1.1 copy-done.7
  73.1 14.3 %rows_to_heads.1.landed = bf16[192,2048]{1,0:T(8,128)(2,1)S(1)} custom-call(bf16[12,192,128]{2,1,0:T(8,128)(2,1)S(1)} %copy-done.7), custom_call_target="tpu_custom_call" | custom-call | tf_op jit(solution)/shard_map/rows_to_heads/pallas_call | solution.py:625
  87.4 0.9 copy-done.2
  88.3 8.0 %attend.1 = (bf16[192,2048]{1,0:T(8,128)(2,1)}, bf16[2048,192]{1,0:T(8,128)(2,1)}, f32[64,2048]{1,0:T(8,128)}, f32[8,2048]{1,0:T(8,128)}, bf16[16,64,128]{2,1,0:T(8,128)(2,1)}) custom-call(bf16[192,2048]{1,0:T(8,128)(2,1)} %copy-done.2), custom_call_target="tpu_custom_call" | custom-call | tf_op jit(solution)/shard_map/attend/pallas_call | solution.py:536
  96.3 0.9 copy-done.9
  97.3 9.0 %heads_to_rows.1 = bf16[12,64,128]{2,1,0:T(8,128)(2,1)S(1)} custom-call(bf16[16,64,128]{2,1,0:T(8,128)(2,1)S(1)} %copy-done.9), custom_call_target="tpu_custom_call" | custom-call | tf_op jit(solution)/shard_map/heads_to_rows/pallas_call | solution.py:625
  106.9 19.0 %feed_forward_both_ways.1 = (f32[128,768]{1,0:T(8,128)}, f32[128,768]{1,0:T(8,128)}, bf16[768,128]{1,0:T(8,128)(2,1)}, bf16[30,768,128]{2,1,0:T(8,128)(2,1)}, bf...) custom-call(f32[128,768]{1,0:T(8,128)} %bitcast.46, f32[128,768]{1,0:T(8,128)} %bitcast.50, ...), custom_call_target="tpu_custom_call" | custom-call | tf_op jit(solution)/shard_map/feed_forward_both_ways/pallas_call | solution.py:536
  126.0 0.9 copy-done.10
  126.9 9.1 %gradient_to_heads.1.landed = bf16[64,2048]{1,0:T(8,128)(2,1)S(1)} custom-call(bf16[12,64,128]{2,1,0:T(8,128)(2,1)S(1)} %bitcast.40), custom_call_target="tpu_custom_call" | custom-call | tf_op jit(solution)/shard_map/gradient_to_heads/pallas_call | solution.py:625
  136.7 9.7 %attend_back.1.blocks = bf16[16,192,128]{2,1,0:T(8,128)(2,1)} custom-call(bf16[192,2048]{1,0:T(8,128)(2,1)} %get-tuple-element.44.ordered, bf16[2048,192]{1,0:T(8,128)(2,1)} %get-tuple-element.45.natural, f32[64,2048]{1,0:T(8,128)} %get-tuple-element.46.out_t, f32[8,2048]{1,0:T(8,128)} %get-tuple-element.47.log_total, bf16[64,2048]{1,0:T(8,128)(2,1)} %copy-done.5), custom_call_target="tpu_custom_call" | custom-call | tf_op jit(solution)/shard_map/attend_back/pallas_call | solution.py:536
  146.5 1.1 copy-done.3
  147.6 14.9 %gradient_to_rows.1.d_qkv_t = bf16[12,192,128]{2,1,0:T(8,128)(2,1)S(1)} custom-call(bf16[16,192,128]{2,1,0:T(8,128)(2,1)S(1)} %copy-done.3), custom_call_target="tpu_custom_call" | custom-call | tf_op jit(solution)/shard_map/gradient_to_rows/pallas_call | solution.py:625
  163.3 7.8 %input_gradient.1 = (f32[128,768]{1,0:T(8,128)}, bf16[18,768,128]{2,1,0:T(8,128)(2,1)}, bf16[128,16,128]{2,1,0:T(8,128)(2,1)}) custom-call(f32[128,768]{1,0:T(8,128)} %bitcast.47, bf16[128,768]{1,0:T(8,128)(2,1)} %get-tuple-element.42.normed, f32[128,768]{1,0:T(8,128)} %get-tuple-element.43.d_middle, bf16[12,192,128]{2,1,0:T(8,128)(2,1)} %copy-done.4, ...), custom_call_target="tpu_custom_call" | custom-call | tf_op jit(solution)/shard_map/input_gradient/pallas_call | solution.py:536
  171.2 6.4 %pad_maximum_fusion = bf16[48,768,128]{2,1,0:T(8,128)(2,1)} fusion(bf16[30,768,128]{2,1,0:T(8,128)(2,1)S(1)} %bitcast.43, bf16[18,768,128]{2,1,0:T(8,128)(2,1)} %get-tuple-element.52), kind=kLoop, calls=%fused_computation | loop fusion | flops 4718592 | bytes 18874368 | tf_op jit(solution)/shard_map/concatenate | solution.py:906
  177.6 67.1 %reduce_grads.1 = (f32[8,6144]{1,0:T(8,128)}, f32[24,768]{1,0:T(8,128)}, f32[16,128]{1,0:T(8,128)}) custom-call(bf16[4,12,2,4,2,48,128]{6,5,4,3,2,1,0:T(8,128)(2,1)} %bitcast.41, bf16[6,2,4,2,4,48,128]{6,5,4,3,2,1,0:T(8,128)(2,1)} %bitcast.44, bf16[2,4,2,4,2,16,128]{6,5,4,3,2,1,0:T(8,128)(2,1)} %bitcast.48, bf16[128,48]{1,0:T(8,128)(2,1)} %constant.20.clone.refs_3_, ...), custom_call_target="tpu_custom_call" | custom-call | tf_op jit(solution)/shard_map/reduce_grads/pallas_call | solution.py:435
  244.7 1.2 slice.27
  245.9 1.2 slice_bitcast_fusion.4
  249.7 0.9 slice_bitcast_fusion.1
  250.6 0.9 slice_bitcast_fusion
  252.9 1.5 copy.36
  (39 shorter events, 11.6 us)
Async XLA Ops:
  3.8 0.7 copy-start.11
  4.5 0.7 copy-start.12
  60.3 3.7 %copy-start = (bf16[4,12,2,4,2,48,128]{6,5,4,3,2,1,0:T(8,128)(2,1)}, bf16[4,12,2,4,2,48,128]{6,5,4,3,2,1,0:T(8,128)(2,1)S(1)}, u32[]{:S(2)}) copy-start(bf16[4,12,2,4,2,48,128]{6,5,4,3,2,1,0:T(8,128)(2,1)S(1)} %get-tuple-element.35) | copy-start | bytes 28311556
  64.0 2.1 copy-start.1
  66.2 0.8 copy-start.8
  72.1 1.1 copy-start.7
  87.4 0.9 copy-start.2
  96.3 0.9 copy-start.9
  106.3 0.7 copy-start.6
  126.0 0.9 copy-start.10
  136.0 0.7 copy-start.5
  146.5 1.1 copy-start.3
  147.6 23.5 %slice-start = ((s8[5898240]{0:T(1024)(128)(4,1)}), s8[4194304]{0:T(1024)(128)(4,1)S(1)}, s32[]{:S(2)}) async-start(s8[5898240]{0:T(1024)(128)(4,1)} %bitcast.42), calls=%async_computation | async-start | bytes 8388608
  162.5 0.8 copy-start.4
  163.3 7.8 %slice-start.1 = ((s8[5898240]{0:T(1024)(128)(4,1)}), s8[1703936]{0:T(1024)(128)(4,1)S(1)}, s32[]{:S(2)}) async-start(s8[5898240]{0:T(1024)(128)(4,1)} %bitcast.42), calls=%async_computation.1 | async-start | bytes 3407872

commit v2 on v0

v2 whole, which is shorter than its diff:
```python
import jax
import jax.numpy as jnp
import numpy as np
from jax import lax
from jax.experimental import pallas as pl
from jax.experimental.pallas import tpu as pltpu
from jax.sharding import PartitionSpec as P

BF = jnp.bfloat16
F32 = jnp.float32
MESH = pl.DeviceIdType.MESH
VMEM = pltpu.VMEM
ALL = slice(None)
AXES = ("x", "y", "z")
GATHER_ORDER = (("x", "y", "z"), ("y", "z", "x"), ("z", "x", "y"))
REDUCE_ORDER = tuple(order[::-1] for order in GATHER_ORDER)
SHAPES = ((4, 6, 2, 4, 2, 48, 128), (4, 12, 2, 4, 2, 48, 128), (2, 4, 2, 4, 2, 16, 128))
SUMS = ((4, 3, 2, 4, 2, 48, 128), (4, 6, 2, 4, 2, 48, 128), (2, 4, 2, 4, 16, 128))
ATTENTION = ((0, 0), (0, 1), (0, 2))
FORWARD = ((1, 0), (1, 1), (1, 2))
SMALL = ((2, 0),)
HEADS = 12
WIDTH = 768
HIDDEN = 3072
NORM_EPS = 1e-05
MASKED = -1e30
MEGA = 1024 * 1024
COPIES = 256


def place():
    dp = lax.axis_index("dp")
    ctx = lax.axis_index("ctx")
    at = {
        "x": lax.rem(lax.div(ctx, 2), 4),
        "y": lax.rem(dp, 4),
        "z": lax.div(ctx, 8) * 2 + lax.div(dp, 4),
    }
    return at, lax.rem(ctx, 2)


def device(at, core):
    return {
        "dp": lax.rem(at["z"], 2) * 4 + at["y"],
        "ctx": lax.div(at["z"], 2) * 8 + at["x"] * 2 + core,
    }


def beside(at, axis, distance):
    moved = dict(at)
    moved[axis] = lax.rem(at[axis] + (distance + 4), 4)
    return moved


def split_z(z):
    if isinstance(z, tuple):
        return pl.ds(z[1], 1), ALL
    if isinstance(z, slice):
        return ALL, ALL
    return lax.rem(z, 2), lax.div(z, 2)


def line(value):
    return pl.ds(2 * value[1], 2) if isinstance(value, tuple) else value


def view(refs, sub, sel, core):
    kind, tile = sub
    x, y = line(sel["x"]), line(sel["y"])
    zl, zh = split_z(sel["z"])
    if kind == 2:
        return refs[2].at[zl, y, zh, x] if core is None else refs[2].at[zl, y, zh, x, core]
    count = kind + 1
    start = count * tile + (0 if core is None else 3 * count * core)
    return refs[kind].at[x, pl.ds(start, count), zl, y, zh]


def block_shape(sub, gone, half_axis=None):
    extent = {axis: 1 if axis in gone else 4 for axis in AXES}
    if half_axis is not None:
        extent[half_axis] = 2
    lead = lambda name: () if extent[name] == 1 else (extent[name],)
    zl, zh = ((), ()) if extent["z"] == 1 else ((extent["z"] // 2,), (2,))
    if sub[0] == 2:
        return zl + lead("y") + zh + lead("x") + (16, 128)
    return lead("x") + (sub[0] + 1,) + zl + lead("y") + zh + (48, 128)


def landing_shapes():
    found = {}
    for sub in ATTENTION + FORWARD + SMALL:
        order = REDUCE_ORDER[sub[1]]
        for phase in range(3):
            gone = order[: phase + 1]
            if phase == 0 and sub[0] < 2:
                for half in range(2):
                    for use in range(3):
                        found[sub, phase, half, use] = block_shape(sub, gone, order[2])
            else:
                for use in range(3):
                    found[sub, phase, use] = block_shape(sub, gone)
    return found


def added(target, *terms):
    if len(target.shape) == 2:
        total = target[...].astype(F32)
        for term in terms:
            total = total + term[...].astype(F32)
        target[...] = total.astype(BF)
        return

    def step(i, carry):
        total = target[i].astype(F32)
        for term in terms:
            total = total + term[i].astype(F32)
        target[i] = total.astype(BF)
        return carry

    lax.fori_loop(0, target.shape[0], step, 0)


class Mail:
    def __init__(self, send_sem, recv_sem, anyone):
        self.send_sem, self.recv_sem, self.anyone = send_sem, recv_sem, anyone
        self.used, self.sent = 0, []

    def send(self, source, target, device_id):
        key = self.used
        copy = pltpu.make_async_remote_copy(
            src_ref=source,
            dst_ref=target,
            send_sem=self.send_sem.at[key],
            recv_sem=self.recv_sem.at[key],
            device_id=device_id,
            device_id_type=MESH,
        )
        copy.start()
        self.sent.append(copy)
        self.used += 1
        return key

    def receive(self, key, arrival):
        pltpu.make_async_remote_copy(
            src_ref=arrival,
            dst_ref=arrival,
            send_sem=self.send_sem.at[key],
            recv_sem=self.recv_sem.at[key],
            device_id=self.anyone,
            device_id_type=MESH,
        ).wait_recv()

    def finish(self):
        for copy in self.sent:
            copy.wait_send()
        self.sent = []


class Gather:
    def __init__(self, mail, refs, subs, at, core):
        self.mail, self.refs, self.subs, self.at, self.core = mail, refs, subs, at, core
        self.twin = device(at, 1 - core)
        self.pending, self.twins = [], []

    def sel(self, sub, phase):
        found = dict(self.at)
        for done in GATHER_ORDER[sub[1]][:phase]:
            found[done] = ALL
        return found

    def mine(self, sub, sel):
        return view(self.refs, sub, sel, self.core)

    def peer(self, axis, distance):
        return device(beside(self.at, axis, distance), self.core)

    def to_twin(self, sub, sel):
        source = self.mine(sub, sel)
        self.twins.append((self.mail.send(source, source, self.twin), view(self.refs, sub, sel, 1 - self.core)))

    def collect(self):
        for wait in self.pending:
            self.mail.receive(*wait)
        self.pending = []

    def straight(self, phase):
        self.collect()
        for sub in self.subs:
            axis, sel = GATHER_ORDER[sub[1]][phase], self.sel(sub, phase)
            source = self.mine(sub, sel)
            for distance in (1, -1, 2):
                key = self.mail.send(source, source, self.peer(axis, distance))
                self.pending.append((key, self.mine(sub, beside(sel, axis, -distance))))

    def ring(self):
        self.collect()
        self.keys = []
        for sub in self.subs:
            axis, sel = GATHER_ORDER[sub[1]][2], self.sel(sub, 2)
            source = self.mine(sub, sel)
            self.keys.append([self.mail.send(source, source, self.peer(axis, d)) for d in (1, -1)])
        for sub in self.subs:
            self.to_twin(sub, self.sel(sub, 2))

    def pass_on(self):
        for sub, keys in zip(self.subs, self.keys):
            order = GATHER_ORDER[sub[1]]
            axis, sel = order[2], self.sel(sub, 2)
            for half, distance in ((0, 1), (1, -1)):
                arrived, far = beside(sel, axis, -distance), beside(sel, axis, 2)
                self.mail.receive(keys[half], self.mine(sub, arrived))
                moving = self.mine(sub, {**arrived, order[0]: ("half", half)})
                coming = self.mine(sub, {**far, order[0]: ("half", half)})
                self.pending.append((self.mail.send(moving, moving, self.peer(axis, distance)), coming))
        for sub in self.subs:
            for distance in (1, -1):
                self.to_twin(sub, beside(self.sel(sub, 2), GATHER_ORDER[sub[1]][2], distance))

    def last(self):
        self.collect()
        for sub in self.subs:
            self.to_twin(sub, beside(self.sel(sub, 2), GATHER_ORDER[sub[1]][2], 2))

    def finish(self):
        for wait in self.twins:
            self.mail.receive(*wait)


class Reduce:
    def __init__(self, mail, sums, landing, subs, at, core):
        self.mail, self.sums, self.landing, self.subs, self.at, self.core = mail, sums, landing, subs, at, core
        self.kept = {}

    def sel(self, sub, phase):
        found = dict(self.at)
        for later in REDUCE_ORDER[sub[1]][phase + 1 :]:
            found[later] = ALL
        return found

    def mine(self, sub, sel, half=None):
        if half is not None:
            sel = {**sel, REDUCE_ORDER[sub[1]][2]: ("half", half)}
        return view(self.sums, sub, sel, None)

    def peer(self, axis, distance):
        return device(beside(self.at, axis, distance), self.core)

    def ring(self):
        for sub in self.subs:
            axis, sel, land = REDUCE_ORDER[sub[1]][0], self.sel(sub, 0), self.landing
            plus, minus = self.peer(axis, 1), self.peer(axis, -1)
            far, up, down = beside(sel, axis, 2), beside(sel, axis, 1), beside(sel, axis, -1)
            self.kept[sub] = [
                self.mail.send(self.mine(sub, far, 0), land[sub, 0, 0, 0], plus),
                self.mail.send(self.mine(sub, far, 1), land[sub, 0, 1, 0], minus),
                self.mail.send(self.mine(sub, up, 1), land[sub, 0, 1, 1], plus),
                self.mail.send(self.mine(sub, down, 0), land[sub, 0, 0, 2], minus),
            ]

    def pass_on(self):
        for sub in self.subs:
            axis, sel, land = REDUCE_ORDER[sub[1]][0], self.sel(sub, 0), self.landing
            keys = self.kept[sub]
            for half, distance in ((0, 1), (1, -1)):
                self.mail.receive(keys[half], land[sub, 0, half, 0])
                moving = self.mine(sub, beside(sel, axis, distance), half)
                added(moving, land[sub, 0, half, 0])
                keys.append(self.mail.send(moving, land[sub, 0, half, 1 + half], self.peer(axis, distance)))

    def collect_ring(self):
        for sub in self.subs:
            sel, land, keys = self.sel(sub, 0), self.landing, self.kept[sub]
            for half, first, second in ((1, keys[2], keys[5]), (0, keys[4], keys[3])):
                self.mail.receive(first, land[sub, 0, half, 1])
                self.mail.receive(second, land[sub, 0, half, 2])
                added(self.mine(sub, sel, half), land[sub, 0, half, 1], land[sub, 0, half, 2])

    def straight(self, phase):
        for sub in self.subs:
            axis, sel = REDUCE_ORDER[sub[1]][phase], self.sel(sub, phase)
            self.kept[sub] = [
                self.mail.send(
                    self.mine(sub, beside(sel, axis, distance)),
                    self.landing[sub, phase, use],
                    self.peer(axis, distance),
                )
                for use, distance in enumerate((1, -1, 2))
            ]

    def collect(self, phase):
        for sub in self.subs:
            terms = [self.landing[sub, phase, use] for use in range(3)]
            for key, term in zip(self.kept[sub], terms):
                self.mail.receive(key, term)
            added(self.mine(sub, self.sel(sub, phase)), *terms)


def dot(left, right):
    return jnp.dot(left, right, preferred_element_type=F32)


def dot_right_t(left, right):
    return lax.dot_general(left, right, (((1,), (1,)), ((), ())), preferred_element_type=F32)


def dot_left_t(left, right):
    return lax.dot_general(left, right, (((0,), (0,)), ((), ())), preferred_element_type=F32)


def flip(values):
    return values.astype(F32).T.astype(BF)


def mean_last(values):
    return jnp.mean(values, axis=-1, keepdims=True)


def sum_rows(values):
    return jnp.sum(values, axis=0, keepdims=True)


def normalize(values):
    center = values - mean_last(values)
    factor = lax.rsqrt(mean_last(center * center) + NORM_EPS)
    return center * factor, factor


def norm_back(d_norm, xhat, factor, gain):
    e = d_norm * gain
    return factor * (e - mean_last(e) - xhat * mean_last(e * xhat))


def owner_mask(shape, column, each):
    owner = lax.broadcasted_iota(jnp.int32, shape, 0) * each
    return (column >= owner) & (column < owner + each)


def width_mask(first):
    shape = (16, 16, WIDTH)
    return owner_mask(shape, lax.broadcasted_iota(jnp.int32, shape, 2) - 6 * first, 6)


def hidden_mask(columns):
    shape = (128, HIDDEN)
    return owner_mask(shape, jnp.broadcast_to(columns, shape), 24)


def low_half(shape):
    return lax.broadcasted_iota(jnp.int32, shape, 1) < 64


def swap_halves(tile):
    return pltpu.roll(tile, 64, 1)


def position_tile(block, tile):
    if tile < 8:
        low, high = block(2 * tile), swap_halves(block(2 * tile + 1))
    else:
        low, high = swap_halves(block(31 - 2 * tile)), block(30 - 2 * tile)
    return jnp.where(low_half(low.shape), low, high)


def position_block(tile, block):
    early, late = tile(block // 2), tile((31 - block) // 2)
    if block % 2 == 0:
        return jnp.where(low_half(early.shape), early, late)
    return swap_halves(jnp.where(low_half(early.shape), late, early))


TILE = 256
KEYS = 1024


def columns_of(tile):
    return slice(128 * tile, 128 * tile + 128)


def causal(scores, first):
    key = lax.broadcasted_iota(jnp.int32, scores.shape, 0)
    query = lax.broadcasted_iota(jnp.int32, scores.shape, 1) + first
    return jnp.where(key <= query, scores, MASKED)


def scores_of(ordered, natural, first, count):
    queries = ordered[0:64, first:count]
    return causal(dot(natural[0:count, :], jnp.concatenate([jnp.zeros_like(queries), queries], axis=0)), first)


def order_heads(landed, ordered, natural):
    for tile in range(16):
        found = position_tile(lambda b: landed[:, columns_of(b)].astype(F32), tile)
        found = jnp.concatenate([found[0:64] * 0.125, found[64:192]], axis=0)
        ordered[:, columns_of(tile)] = found.astype(BF)
        natural[columns_of(tile), :] = found[0:128].T.astype(BF)


def attend(step, ordered, natural, out_t, log_total):
    first = TILE * step
    count = first + TILE
    scores = scores_of(ordered, natural, first, count)
    best = jnp.max(scores, axis=0, keepdims=True)
    probs = jnp.exp(scores - best)
    total = sum_rows(probs)
    out_t[:, first:count] = dot(ordered[128:192, 0:count], probs.astype(BF)) / total
    log_total[0:1, first:count] = best + jnp.log(total)


def order_back(landed, ordered, d_out, values_natural):
    for tile in range(16):
        found = position_tile(lambda b: landed[:, columns_of(b)].astype(F32), tile)
        d_out[:, columns_of(tile)] = found
        both = jnp.concatenate([ordered[128:192, columns_of(tile)].astype(F32), found], axis=0)
        values_natural[columns_of(tile), :] = both.T.astype(BF)


def attend_back(step, ordered, natural, values_natural, out_t, log_total, d_out, d_t, d_keys):
    first = TILE * step
    count = first + TILE
    queries = ordered[0:64, first:count]
    queries = jnp.concatenate([jnp.zeros_like(queries), queries], axis=0)
    log_here = log_total[0:1, first:count]
    d_here = d_out[:, first:count]
    delta = sum_rows(d_here * out_t[:, first:count])
    d_low = d_here.astype(BF)
    d_low = jnp.concatenate([d_low, jnp.zeros_like(d_low)], axis=0)
    query_rows, d_rows = natural[first:count, :], values_natural[first:count, :]
    low = low_half(query_rows.shape)
    query_rows = jnp.where(low, query_rows, jnp.zeros_like(query_rows))
    d_rows = jnp.where(low, jnp.zeros_like(d_rows), d_rows)
    d_query = jnp.zeros((64, TILE), F32)
    for begin in range(0, count, KEYS):
        end = min(begin + KEYS, count)
        scores = dot(natural[begin:end, :], queries)
        if end == count:
            scores = causal(scores, first - begin)
        probs = jnp.exp(scores - log_here)
        d_scores = (probs * (dot(values_natural[begin:end, :], d_low) - delta)).astype(BF)
        d_query = d_query + dot(ordered[64:128, begin:end], d_scores)
        update = dot(d_scores, query_rows) + dot(probs.astype(BF), d_rows)
        if begin < first:
            done = min(end, first)
            d_keys[begin:done, :] += update[: done - begin]
        if end == count:
            d_keys[first:count, :] = update[first - begin :]
    d_t[0:64, first:count] = d_query * 0.125


def layer_kernel(*refs):
    shapes = landing_shapes()
    (
        x, cotangent, w_joint, w_proj, w_small, place_q, place_p, spread_q, spread_p, spread, spread_fc, columns,
        final, input_grad, out_q, out_fc, out_p, out_v,
    ) = refs[:18]
    weights, grads, sums = refs[18:21], refs[21:24], refs[24:27]
    landing = dict(zip(shapes, refs[27 : 27 + len(shapes)]))
    (
        in_joint, in_proj, last_q, last_fc, last_p, back_q, back_fc, back_p,
        normed, vectors, hidden_bias, qkv_t, landed, ordered, natural, out_t, log_total, att_blocks, att_t,
        total, d_norm_two, d_middle, d_att_t, landed_back, d_out, values_natural, d_t, d_keys, d_blocks,
        d_rows, d_qkv, grad_vectors, grad_hidden,
        send_sem, recv_sem, head_send, head_recv, local_sem,
    ) = refs[27 + len(shapes) :]
    at, core = place()
    ctx = lax.axis_index("ctx")
    spot = at["x"] * 2 + core
    is_head = ctx < HEADS
    twin = device(at, 1 - core)
    mail = Mail(send_sem, recv_sem, twin)

    known = [{"ctx": lax.rem(ctx + step, 16)} for step in range(1, 16)]
    known += [device(beside(at, "y", distance), core) for distance in (1, -1, 2)]
    known += [device(beside(at, "z", distance), core) for distance in (1, -1)]
    barrier = pltpu.get_barrier_semaphore()
    for target in known:
        pl.semaphore_signal(barrier, inc=1, device_id=target, device_id_type=MESH)
    pl.semaphore_wait(barrier, len(known))

    def group_sends(source, target):
        waits = []
        for step in range(1, 8):
            other = lax.rem(spot + step, 8)
            origin = lax.rem(spot + 8 - step, 8)
            peer = device({**at, "x": lax.div(other, 2)}, lax.rem(other, 2))
            waits.append((mail.send(source.at[other], target.at[spot], peer), target.at[origin]))
        target[spot] = source[spot]
        return waits

    def pair_sends(source, target):
        key = mail.send(source.at[1 - core], target.at[core], twin)
        target[core] = source[core]
        return [(key, target.at[1 - core])]

    def receive(waits):
        for wait in waits:
            mail.receive(*wait)

    def head_span(ref, who):
        return ref.at[:, pl.ds(pl.multiple_of(who * 128, 128), 128)]

    def head_copy(turn, step, source, target, peer):
        return pltpu.make_async_remote_copy(
            source, target, head_send.at[turn, step], head_recv.at[turn, step],
            device_id={"ctx": peer}, device_id_type=MESH,
        )

    def to_heads(turn, block, out):
        for step in range(1, 16):
            peer = lax.rem(ctx + step, 16)

            @pl.when(peer < HEADS)
            def _():
                head_copy(turn, step, block.at[peer], head_span(out, ctx), peer).start()

        @pl.when(is_head)
        def _():
            pltpu.make_async_copy(block.at[ctx], head_span(out, ctx), local_sem.at[turn]).start()

    def to_heads_received(turn, block, out):
        @pl.when(is_head)
        def _():
            for step in range(1, 16):
                source = lax.rem(ctx + 16 - step, 16)
                head_copy(turn, step, head_span(out, source), head_span(out, source), source).wait_recv()
            pltpu.make_async_copy(block.at[ctx], head_span(out, ctx), local_sem.at[turn]).wait()

    def to_heads_sent(turn, block, out):
        for step in range(1, 16):
            peer = lax.rem(ctx + step, 16)

            @pl.when(peer < HEADS)
            def _():
                head_copy(turn, step, block.at[peer], head_span(out, ctx), peer).wait_send()

    def from_heads(turn, blocks, out):
        @pl.when(is_head)
        def _():
            for step in range(1, 16):
                peer = lax.rem(ctx + step, 16)
                head_copy(turn, step, blocks.at[peer], out.at[ctx], peer).start()
            pltpu.make_async_copy(blocks.at[ctx], out.at[ctx], local_sem.at[turn]).start()

    def from_heads_received(turn, blocks, out):
        for step in range(1, 16):
            source = lax.rem(ctx + 16 - step, 16)

            @pl.when(source < HEADS)
            def _():
                head_copy(turn, step, out.at[source], out.at[source], source).wait_recv()

        @pl.when(is_head)
        def _():
            pltpu.make_async_copy(blocks.at[ctx], out.at[ctx], local_sem.at[turn]).wait()

    def from_heads_sent(turn, blocks, out):
        @pl.when(is_head)
        def _():
            for step in range(1, 16):
                peer = lax.rem(ctx + step, 16)
                head_copy(turn, step, blocks.at[peer], out.at[ctx], peer).wait_send()

    zl, zh = split_z(at["z"])
    waits = group_sends(w_joint, in_joint) + pair_sends(w_proj, in_proj)
    weights[2][zl, at["y"], zh, at["x"], core] = w_small[...]
    receive(waits)
    rows = dot(place_q[...], in_joint[...].reshape(128, WIDTH)).astype(BF)
    proj_rows = dot(place_p[...], in_proj[...].reshape(64, 384)).astype(BF)
    for tile in range(3):
        span = columns_of(tile)
        weights[0][at["x"], 3 * core + tile, zl, at["y"], zh] = rows[:, span]
        weights[1][at["x"], 6 * core + 2 * tile, zl, at["y"], zh] = rows[:, 384 + 128 * tile : 512 + 128 * tile]
        weights[1][at["x"], 6 * core + 2 * tile + 1, zl, at["y"], zh] = proj_rows[:, span]

    first = Gather(mail, weights, ATTENTION + SMALL, at, core)
    second = Gather(mail, weights, FORWARD, at, core)
    first.straight(0)
    second.straight(0)
    first.straight(1)
    second.straight(1)
    first.ring()
    xhat, _ = normalize(x[...])
    first.pass_on()
    second.ring()
    first.last()
    first.finish()

    small_rows = weights[2][...].reshape(2048, 128)
    found = jnp.zeros((16, WIDTH), F32)
    for group in range(8):
        wide = dot(small_rows[256 * group : 256 * group + 256], spread[...]).reshape(16, 16, WIDTH)
        found = found + jnp.sum(jnp.where(width_mask(16 * group), wide, 0.0), axis=0)
    vectors[...] = found
    tall = small_rows.astype(F32).reshape(128, 16, 128)
    eighth = lax.broadcasted_iota(jnp.int32, (128, 16, 128), 1) == 8
    fc_rows = jnp.sum(jnp.where(eighth, tall, 0.0), axis=1).astype(BF)
    hidden_bias[...] = sum_rows(jnp.where(hidden_mask(columns[...]), dot(fc_rows, spread_fc[...]), 0.0))
    normed_rows = (xhat * vectors[0:1] + vectors[2:3]).astype(BF)
    normed[...] = normed_rows

    def joint_tiles(start, count):
        tiles = [weights[0][t // 6, t % 6].reshape(WIDTH, 128) for t in range(start, start + count)]
        return jnp.concatenate(tiles, axis=1)

    for pair in range(9):
        kind, offset = pair // 3, (pair % 3) * 256
        out = dot(normed_rows, joint_tiles(2 * pair, 2))
        if kind != 1:
            out = out + vectors[3 + kind // 2 : 4 + kind // 2, offset : offset + 256]
        out = flip(out.astype(BF))
        for head in range(4):
            qkv_t[offset // 64 + head, 64 * kind : 64 * kind + 64, :] = out[64 * head : 64 * head + 64]
    to_heads(0, qkv_t, landed)
    second.pass_on()
    to_heads_received(0, qkv_t, landed)

    @pl.when(is_head)
    def _():
        order_heads(landed, ordered, natural)
        for step in range(4):
            attend(step, ordered, natural, out_t, log_total)

    second.last()

    @pl.when(is_head)
    def _():
        for step in range(4, 2048 // TILE):
            attend(step, ordered, natural, out_t, log_total)
        for block in range(16):
            att_blocks[block] = position_block(lambda t: out_t[:, columns_of(t)], block).astype(BF)

    from_heads(1, att_blocks, att_t)
    second.finish()
    from_heads_received(1, att_blocks, att_t)

    rows_t = att_t[...].reshape(WIDTH, 128)
    mat_out = joint_tiles(18, 6)
    middle = x[...] + dot(flip(rows_t), mat_out) + vectors[5:6]
    xhat, factor = normalize(middle)
    normed_two = (xhat * vectors[1:2] + vectors[6:7]).astype(BF)
    normed_t = flip(normed_two)
    gradient = cotangent[...]
    d_two = gradient.astype(BF)
    d_norm = jnp.zeros((128, WIDTH), F32)
    twin_waits = {}
    for chunk in range(4):
        tile = lambda half, t: weights[1][chunk, 2 * t + half].reshape(WIDTH, 128)
        mat_fc = jnp.concatenate([tile(0, t) for t in range(6)], axis=1)
        mat_proj = jnp.concatenate([tile(1, t) for t in range(6)], axis=1)
        span = slice(WIDTH * chunk, WIDTH * chunk + WIDTH)
        pre = dot(normed_two, mat_fc) + hidden_bias[:, span]
        root = 0.7978845608028654
        inner = jnp.tanh(root * (pre + 0.044715 * (pre * pre * pre)))
        activated = (0.5 * pre * (1.0 + inner)).astype(BF)
        slope = 0.5 * (1.0 + inner) + 0.5 * pre * (1.0 - inner * inner) * (
            root * (1.0 + 3 * 0.044715 * (pre * pre))
        )
        update = dot(activated, mat_proj)
        total[...] = update if chunk == 0 else total[...] + update
        d_pre = (dot_right_t(d_two, mat_proj) * slope).astype(BF)
        grad_hidden[:, span] = sum_rows(d_pre.astype(F32))
        update = dot_right_t(d_pre, mat_fc)
        d_norm_two[...] = update if chunk == 0 else d_norm_two[...] + update
        grad_fc = dot(normed_t, d_pre).astype(BF)
        grad_proj = dot_left_t(activated, d_two).astype(BF)
        for t in range(6):
            grads[1][chunk, 2 * t] = grad_fc[:, columns_of(t)].reshape(2, 4, 2, 48, 128)
            grads[1][chunk, 2 * t + 1] = grad_proj[:, columns_of(t)].reshape(2, 4, 2, 48, 128)
        key = mail.send(grads[1].at[chunk, pl.ds(6 * (1 - core), 6)], sums[1].at[chunk], twin)
        twin_waits[1, chunk] = key
    final[...] = middle + total[...] + vectors[7:8]
    d_norm = d_norm_two[...]
    d_mid = gradient + norm_back(d_norm, xhat, factor, vectors[1:2])
    d_middle[...] = d_mid
    d_one = d_mid.astype(BF)
    d_att_t[...] = dot_right_t(mat_out, d_one).astype(BF).reshape(HEADS, 64, 128)
    to_heads(2, d_att_t, landed_back)
    grad_out = dot(rows_t, d_one).astype(BF)
    for t in range(6):
        grads[0][3, t] = grad_out[:, columns_of(t)].reshape(2, 4, 2, 48, 128)
    twin_waits[0, 3] = mail.send(grads[0].at[3, pl.ds(3 * (1 - core), 3)], sums[0].at[3], twin)
    grad_vectors[...] = jnp.zeros_like(grad_vectors)
    grad_vectors[1:2] = sum_rows(d_norm * xhat)
    grad_vectors[5:6] = sum_rows(d_one.astype(F32))
    grad_vectors[6:7] = sum_rows(d_norm)
    grad_vectors[7:8] = sum_rows(d_two.astype(F32))

    def add_twin(kind, chunk):
        mail.receive(twin_waits[kind, chunk], sums[kind].at[chunk])
        count = 3 * (kind + 1)
        added(sums[kind].at[chunk], grads[kind].at[chunk, pl.ds(count * core, count)])

    back_second = Reduce(mail, sums, landing, FORWARD, at, core)
    for chunk in range(4):
        add_twin(1, chunk)
    back_second.ring()
    add_twin(0, 3)

    to_heads_received(2, d_att_t, landed_back)

    @pl.when(is_head)
    def _():
        order_back(landed_back, ordered, d_out, values_natural)
        for step in range(5):
            attend_back(step, ordered, natural, values_natural, out_t, log_total, d_out, d_t, d_keys)

    back_second.pass_on()

    @pl.when(is_head)
    def _():
        for step in range(5, 2048 // TILE):
            attend_back(step, ordered, natural, values_natural, out_t, log_total, d_out, d_t, d_keys)
        for tile in range(16):
            d_t[64:192, columns_of(tile)] = d_keys[columns_of(tile), :].T
        for block in range(16):
            d_blocks[block] = position_block(lambda t: d_t[:, columns_of(t)], block).astype(BF)

    from_heads(3, d_blocks, d_rows)
    back_second.collect_ring()
    back_second.straight(1)
    from_heads_received(3, d_blocks, d_rows)

    for head in range(HEADS):
        rows = flip(d_rows[head])
        for kind in range(3):
            offset = WIDTH * kind + 64 * head
            d_qkv[:, offset : offset + 64] = rows[:, 64 * kind : 64 * kind + 64]
    normed_t = flip(normed[...])
    for pair in range(9):
        out = dot(normed_t, d_qkv[:, 256 * pair : 256 * pair + 256]).astype(BF)
        for t in range(2):
            tile = 2 * pair + t
            grads[0][tile // 6, tile % 6] = out[:, columns_of(t)].reshape(2, 4, 2, 48, 128)
        if pair % 3 == 2:
            chunk = pair // 3
            source = grads[0].at[chunk, pl.ds(3 * (1 - core), 3)]
            twin_waits[0, chunk] = mail.send(source, sums[0].at[chunk], twin)
    back_second.collect(1)
    back_second.straight(2)
    d_norm = jnp.zeros((128, WIDTH), F32)
    for pair in range(9):
        d_norm = d_norm + dot_right_t(d_qkv[:, 256 * pair : 256 * pair + 256], joint_tiles(2 * pair, 2))
    back_first = Reduce(mail, sums, landing, ATTENTION, at, core)
    for chunk in range(3):
        add_twin(0, chunk)
    back_first.ring()
    xhat, factor = normalize(x[...])
    input_grad[...] = d_middle[...] + norm_back(d_norm, xhat, factor, vectors[0:1])
    kinds = lambda kind: sum_rows(d_qkv[:, WIDTH * kind : WIDTH * kind + WIDTH].astype(F32))
    row = lax.broadcasted_iota(jnp.int32, (16, WIDTH), 0)
    found = grad_vectors[...]
    for which, value in ((0, sum_rows(d_norm * xhat)), (2, sum_rows(d_norm)), (3, kinds(0)), (4, kinds(2))):
        found = jnp.where(row == which, value, found)
    small = []
    for group in range(8):
        wide = jnp.where(width_mask(16 * group), jnp.broadcast_to(found[None], (16, 16, WIDTH)), 0.0)
        small.append(dot_right_t(wide.astype(BF).reshape(256, WIDTH), spread[...]).reshape(16, 16, 128))
    small = jnp.concatenate(small, axis=0)
    wide = jnp.where(hidden_mask(columns[...]), jnp.broadcast_to(grad_hidden[...], (128, HIDDEN)), 0.0)
    hidden = dot_right_t(wide.astype(BF), spread_fc[...])
    eighth = lax.broadcasted_iota(jnp.int32, (128, 16, 128), 1) == 8
    small = jnp.where(eighth, hidden[:, None, :], small)
    grads[2][...] = small.astype(BF).reshape(SHAPES[2])
    every = {axis: ALL for axis in AXES}
    key = mail.send(view(grads, (2, 0), every, 1 - core), sums[2], twin)

    back_second.collect(2)
    mine = [view(sums, sub, at, None) for sub in FORWARD]
    rows = jnp.concatenate([mine[t][0] for t in range(3)], axis=1)
    last_fc[...] = dot(spread_q[...], rows).astype(BF).reshape(8, 16, 384)
    rows = jnp.concatenate([mine[t][1] for t in range(3)], axis=1)
    last_p[...] = dot(spread_p[...], rows).astype(BF).reshape(2, 32, 384)
    waits = group_sends(last_fc, back_fc) + pair_sends(last_p, back_p)
    mail.receive(key, sums[2])
    added(sums[2], view(grads, (2, 0), every, core))
    back_small = Reduce(mail, sums, landing, SMALL, at, core)
    back_small.straight(0)

    back_first.pass_on()
    back_small.collect(0)
    back_small.straight(1)
    back_first.collect_ring()
    back_first.straight(1)
    back_small.collect(1)
    back_small.straight(2)
    receive(waits)
    for group in range(8):
        out_fc[:, 384 * group : 384 * group + 384] = back_fc[group].astype(F32)[:8]
    for half in range(2):
        out_p[:, 384 * half : 384 * half + 384] = back_p[half].astype(F32)[:24]
    back_first.collect(1)
    back_first.straight(2)
    back_small.collect(2)
    out_v[...] = view(sums, (2, 0), at, None)[...].astype(F32)
    back_first.collect(2)
    rows = jnp.concatenate([view(sums, sub, at, None)[0] for sub in ATTENTION], axis=1)
    last_q[...] = dot(spread_q[...], rows).astype(BF).reshape(8, 16, 384)
    receive(group_sends(last_q, back_q))
    for group in range(8):
        out_q[:, 384 * group : 384 * group + 384] = back_q[group].astype(F32)[:8]

    mail.finish()
    to_heads_sent(0, qkv_t, landed)
    from_heads_sent(1, att_blocks, att_t)
    to_heads_sent(2, d_att_t, landed_back)
    from_heads_sent(3, d_blocks, d_rows)


def place_rows(groups, rows, padded):
    found = np.zeros((groups * rows, groups * padded), np.float32)
    for group in range(groups):
        for row in range(rows):
            found[group * rows + row, group * padded + row] = 1
    return found


def spread_matrix(entries, each):
    found = np.zeros((128, len(entries)), np.float32)
    found[entries % each, np.arange(len(entries))] = 1
    return found


def hidden_order():
    x, group, row = np.meshgrid(np.arange(4), np.arange(16), np.arange(48), indexing="ij")
    return (192 * group + 48 * x + row).reshape(-1)


def local(tokens, cotangent, w_qkv, w_out, w_fc, w_proj, gains, biases, fc_bias):
    first = jnp.concatenate([w_qkv[0], w_out[0]], axis=1).reshape(6, 8, 384)
    hidden = jnp.transpose(w_fc[0].reshape(6, 16, 4, 48), (0, 2, 1, 3)).reshape(6, 8, 384)
    joint = jnp.transpose(jnp.concatenate([first, hidden], axis=2), (1, 0, 2))
    joint = jnp.pad(joint, ((0, 0), (0, 10), (0, 0)))
    proj = jnp.pad(jnp.transpose(w_proj[0].reshape(24, 2, 384), (1, 0, 2)), ((0, 0), (0, 8), (0, 0)))
    small = jnp.pad(jnp.concatenate([gains[0], biases[0]], axis=0), ((0, 0), (0, 122)))
    small = jnp.concatenate([small, jnp.pad(fc_bias, ((0, 0), (0, 104))), jnp.zeros((7, 128), BF)], axis=0)
    order = hidden_order()
    scratch = [VMEM(shape, BF) for shape in SHAPES + SHAPES + SUMS + tuple(landing_shapes().values())]
    scratch += [
        VMEM((8, 16, WIDTH), BF),
        VMEM((2, 32, 384), BF),
        VMEM((8, 16, 384), BF),
        VMEM((8, 16, 384), BF),
        VMEM((2, 32, 384), BF),
        VMEM((8, 16, 384), BF),
        VMEM((8, 16, 384), BF),
        VMEM((2, 32, 384), BF),
        VMEM((128, WIDTH), BF),
        VMEM((16, WIDTH), F32),
        VMEM((1, HIDDEN), F32),
        VMEM((HEADS, 192, 128), BF),
        VMEM((192, 2048), BF),
        VMEM((192, 2048), BF),
        VMEM((2048, 128), BF),
        VMEM((64, 2048), F32),
        VMEM((8, 2048), F32),
        VMEM((16, 64, 128), BF),
        VMEM((HEADS, 64, 128), BF),
        VMEM((128, WIDTH), F32),
        VMEM((128, WIDTH), F32),
        VMEM((128, WIDTH), F32),
        VMEM((HEADS, 64, 128), BF),
        VMEM((64, 2048), BF),
        VMEM((64, 2048), F32),
        VMEM((2048, 128), BF),
        VMEM((192, 2048), F32),
        VMEM((2048, 128), F32),
        VMEM((16, 192, 128), BF),
        VMEM((HEADS, 192, 128), BF),
        VMEM((128, 3 * WIDTH), BF),
        VMEM((16, WIDTH), F32),
        VMEM((1, HIDDEN), F32),
        pltpu.SemaphoreType.DMA((COPIES,)),
        pltpu.SemaphoreType.DMA((COPIES,)),
        pltpu.SemaphoreType.DMA((4, 16)),
        pltpu.SemaphoreType.DMA((4, 16)),
        pltpu.SemaphoreType.DMA((4,)),
    ]
    outs = ((128, WIDTH), (128, WIDTH), (8, HIDDEN), (8, HIDDEN), (24, WIDTH), (16, 128))
    final, input_grad, out_q, out_fc, out_p, out_v = pl.pallas_call(
        layer_kernel,
        out_shape=[jax.ShapeDtypeStruct(shape, F32) for shape in outs],
        in_specs=[pl.BlockSpec(memory_space=VMEM)] * 12,
        out_specs=[pl.BlockSpec(memory_space=VMEM)] * 6,
        scratch_shapes=scratch,
        compiler_params=pltpu.CompilerParams(
            collective_id=0, has_side_effects=True, vmem_limit_bytes=VMEM_LIMIT * MEGA
        ),
        name="layer",
    )(
        tokens[0],
        cotangent[0],
        joint,
        proj,
        small,
        jnp.asarray(place_rows(8, 6, 16), BF),
        jnp.asarray(place_rows(2, 24, 32), BF),
        jnp.asarray(place_rows(8, 6, 16).T, BF),
        jnp.asarray(place_rows(2, 24, 32).T, BF),
        jnp.asarray(spread_matrix(np.arange(WIDTH), 6), BF),
        jnp.asarray(spread_matrix(order, 24), BF),
        jnp.asarray(order.reshape(1, HIDDEN), jnp.int32),
    )
    grad_fc = jnp.transpose(out_fc[:6].reshape(6, 4, 16, 48), (0, 2, 1, 3)).reshape(1, 6, HIDDEN)
    return (
        final[None],
        input_grad[None],
        out_q[None, :6, : 3 * WIDTH],
        out_q[None, :6, 3 * WIDTH :],
        grad_fc,
        out_p[None],
        out_v[None, 0:2, :6],
        out_v[None, 2:8, :6],
        out_v[8:9, :24],
    )


VMEM_LIMIT = 63


def solution(mesh):
    rows = P("dp", "ctx", None)
    weight = P(None, ("dp", "ctx"), None)
    vector = P(None, None, ("dp", "ctx"))
    tail = (weight,) * 4 + (vector, vector, P(None, ("dp", "ctx")))
    return jax.shard_map(
        local, mesh=mesh, in_specs=(rows, rows) + tail, out_specs=(rows, rows) + tail, check_vma=False
    )
```

time: 2030 us -> 161 us (0.08)
  blocking collectives: 865 us -> 0 us
  waiting for transfers between devices: 579 us -> 0 us
  starting transfers between devices: 284 us -> 0 us
  Pallas kernels: 0 us -> 143 us
  local copies, waits for them, and re-layouts: 153 us -> 15 us
  matrix products: 85.7 us -> 0 us
  other arithmetic: 24 us -> 0.71 us
    unnamed x3 -> x0, blocking collectives: 512 us -> none
    all_gather x2 -> x0, blocking collectives: 353 us -> none  [the longest x1 181 us: fetch_layer(): lax.all_gather(biases[layer_idx], ('dp', 'ctx'), axis=1, tiled=True)]
    ppermute x46 -> x0, waiting for transfers between devices: 345 us -> none  [from_behind(): return lax.ppermute(block, axis, route)]
    unnamed x96 -> x0, starting transfers between devices: 267 us -> none
    all_gather x4 -> x0, waiting for transfers between devices: 233 us -> none  [the longest x1 193 us: fetch_layer(): lax.all_gather(w_proj[layer_idx], ('dp', 'ctx'), axis=0, tiled=True)]
    pallas_call x0 -> x1, Pallas kernels: none -> 143 us  [local(): pl.pallas_call(layer_kernel, out_shape=[jax.ShapeDtypeStruct(shape, F32)...]
    unnamed x293 -> x26, local copies, waits for them, and re-layouts: 129 us -> 6.69 us
    dot_general x123 -> x0, matrix products: 85.7 us -> none  [the longest x4 15.9 us: rows_product(): lax.dot_general(left, right, (((0,), (0,)), ((), ())), preferred_element_...]
  transfers between devices with their start and end apart: 147 -> 0, of which waited for: 35 -> 0; matrix products, arithmetic and copies ran while one was open for 30% -> 0% of each run, Pallas kernels for 0% -> 0%
where the time goes in v2:
time: 161 us; the launch traced here: 160 us
  Pallas kernels  143 us (89%)
  local copies, waits for them, and re-layouts  15 us (9%)
    pallas_call x1, Pallas kernels, local(): pl.pallas_call(layer_kernel, out_shape=[jax.ShapeDtypeStruct(shape, F32)...  143 us
    unnamed x26, local copies, waits for them, and re-layouts  6.69 us

profile of v2, /device:TPU:1, one launch (start us, length us, event | category | flops | bytes accessed | tf_op | source)
XLA Modules:
  0.0 159.8 jit_solution(2407966379288793524)
XLA Ops:
  0.6 0.9 reshape_squeeze.6
  1.6 0.1 reshape.31
  1.8 0.7 copy-done.4
  2.6 0.7 pad.16.refs_2_
  3.4 0.6 pad.17.refs_3_
  4.0 0.7 copy-done.7
  4.8 0.6 copy-done.8
  5.3 0.7 fusion.3.refs_4_
  6.0 143.4 %layer.1 = (f32[128,768]{1,0:T(8,128)}, f32[128,768]{1,0:T(8,128)}, f32[8,3072]{1,0:T(8,128)}, f32[8,3072]{1,0:T(8,128)}, f32[24,768]{1,0:T(8,128)}, /*index=5*/f32[16,128]{1,0:T(8,128)}) custom-call(f32[128,768]{1,0:T(8,128)} %bitcast.31, f32[128,768]{1,0:T(8,128)} %bitcast.32, bf16[8,16,768]{2,1,0:T(8,128)(2,1)} %pad.16.refs_2_, ...), custom_call_target="tpu_custom_call" | custom-call | tf_op jit(solution)/shard_map/layer/pallas_call | solution.py:878
  149.4 0.7 slice_bitcast_fusion.2
  150.1 0.6 copy.35
  150.6 1.2 slice_bitcast_fusion.3
  151.9 1.2 slice.23
  153.1 0.9 slice_bitcast_fusion
  154.0 0.7 copy.33
  154.6 0.7 slice_bitcast_fusion.1
  155.4 0.6 copy.34
  156.0 0.1 reshape.32
  156.2 0.9 reshape.33
  157.1 0.7 copy.43
  157.9 0.4 copy-done
  158.3 0.7 copy.44
  159.0 0.2 copy-done.3
  159.2 0.6 copy.45
  (25 shorter events, 0.4 us)
Async XLA Ops:
  1.7 0.8 copy-start.4
  1.7 0.8 copy-start.6
  2.5 0.8 copy-start.5
  4.0 0.7 copy-start.7
  4.0 0.7 copy-start.9
  4.7 0.7 copy-start.8
  154.0 2.0 %copy-start.2 = (f32[8,3072]{1,0:T(8,128)S(1)}, f32[8,3072]{1,0:T(8,128)}, u32[]{:S(2)}) copy-start(f32[8,3072]{1,0:T(8,128)} %get-tuple-element.18) | copy-start | bytes 294916
  156.1 1.0 copy-start.1
  157.1 1.1 copy-start
  158.3 0.9 copy-start.3

commit v3 on v2

--- a/solution.py
+++ b/solution.py
@@ -46,6 +46,12 @@
     }
 
 
+def head_at(ctx, z_lo):
+    z_hi, x, core = lax.div(ctx, 8), lax.rem(lax.div(ctx, 2), 4), lax.rem(ctx, 2)
+    head = (1 - core) * (4 * z_hi + x) + core * (8 + 2 * z_hi + x - 2 * z_lo)
+    return (core == 0) | (lax.div(x, 2) == z_lo), head
+
+
 def beside(at, axis, distance):
     moved = dict(at)
     moved[axis] = lax.rem(at[axis] + (distance + 4), 4)
@@ -409,7 +415,7 @@
 def order_back(landed, ordered, d_out, values_natural):
     for tile in range(16):
         found = position_tile(lambda b: landed[:, columns_of(b)].astype(F32), tile)
-        d_out[:, columns_of(tile)] = found
+        d_out[:, columns_of(tile)] = found.astype(BF)
         both = jnp.concatenate([ordered[128:192, columns_of(tile)].astype(F32), found], axis=0)
         values_natural[columns_of(tile), :] = both.T.astype(BF)
 
@@ -420,9 +426,8 @@
     queries = ordered[0:64, first:count]
     queries = jnp.concatenate([jnp.zeros_like(queries), queries], axis=0)
     log_here = log_total[0:1, first:count]
-    d_here = d_out[:, first:count]
-    delta = sum_rows(d_here * out_t[:, first:count])
-    d_low = d_here.astype(BF)
+    d_low = d_out[:, first:count]
+    delta = sum_rows(d_low.astype(F32) * out_t[:, first:count])
     d_low = jnp.concatenate([d_low, jnp.zeros_like(d_low)], axis=0)
     query_rows, d_rows = natural[first:count, :], values_natural[first:count, :]
     low = low_half(query_rows.shape)
@@ -443,28 +448,96 @@
             d_keys[begin:done, :] += update[: done - begin]
         if end == count:
             d_keys[first:count, :] = update[first - begin :]
-    d_t[0:64, first:count] = d_query * 0.125
+    d_t[0:64, first:count] = (d_query * 0.125).astype(BF)
+
+
+def hidden_order():
+    x, group, row = np.meshgrid(np.arange(4), np.arange(16), np.arange(48), indexing="ij")
+    return (192 * group + 48 * x + row).reshape(-1)
+
+
+def reorder(source, order, store):
+    for tile in range(len(order) // 128):
+        wanted = order[columns_of(tile)]
+        lanes = lax.broadcasted_iota(jnp.int32, (8, 128), 1)
+        found = jnp.zeros((8, 128), F32)
+        begin = 0
+        while begin < 128:
+            end = begin + 1
+            while end < 128 and wanted[end] == wanted[end - 1] + 1 and wanted[end] % 128:
+                end += 1
+            at = int(wanted[begin])
+            piece = source[0:8, columns_of(at // 128)]
+            shift = (begin - at) % 128
+            if shift:
+                piece = pltpu.roll(piece, shift, 1)
+            found = jnp.where((lanes >= begin) & (lanes < end), piece, found)
+            begin = end
+        store(tile, found)
+
+
+def results_kernel(
+    final, input_grad, joint, hidden, proj, small,
+    to_final, to_input, to_qkv, to_out, to_fc, to_proj, to_gains, to_biases, to_fc_bias,
+    joint_here, hidden_here, small_here, qkv, out, fc, gains, biases, fc_bias, in_sem, out_sem,
+):
+    straight = [
+        pltpu.make_async_copy(source, target, out_sem.at[i])
+        for i, (source, target) in enumerate(((final, to_final), (input_grad, to_input), (proj, to_proj)))
+    ]
+    loads = [
+        pltpu.make_async_copy(source, target, in_sem.at[i])
+        for i, (source, target) in enumerate(((joint, joint_here), (hidden, hidden_here), (small, small_here)))
+    ]
+    for copy in loads + straight:
+        copy.start()
+    for copy in loads:
+        copy.wait()
+    for row in range(6):
+        qkv[row] = joint_here[row : row + 1, 0 : 3 * WIDTH]
+        out[row] = joint_here[row : row + 1, 3 * WIDTH : HIDDEN]
+        fc[row] = hidden_here[row : row + 1, :]
+        biases[row] = small_here[2 + row : 3 + row, 0:6]
+    gains[...] = small_here[0:2, 0:6]
+    fc_bias[...] = small_here[8:9, 0:24]
+    pairs = ((qkv, to_qkv), (out, to_out), (fc, to_fc), (gains, to_gains), (biases, to_biases), (fc_bias, to_fc_bias))
+    last = [pltpu.make_async_copy(source, target, out_sem.at[3 + i]) for i, (source, target) in enumerate(pairs)]
+    for copy in last:
+        copy.start()
+    for copy in straight + last:
+        copy.wait()
 
 
 def layer_kernel(*refs):
     shapes = landing_shapes()
+    ins, outs, refs = refs[:12], refs[12:18], refs[18:]
+    loaded, refs = refs[:12], refs[12:]
+    x, cotangent, raw_qkv, raw_out, raw_fc, raw_proj, raw_gains, raw_biases, raw_fc_bias, placing, spreads, columns = loaded
+    final, input_grad, out_q, out_fc, out_p, out_v = refs[:6]
+    weights, grads, sums = refs[6:9], refs[9:12], refs[12:15]
+    refs = refs[15:]
+    landing = dict(zip(shapes, refs[: len(shapes)]))
     (
-        x, cotangent, w_joint, w_proj, w_small, place_q, place_p, spread_q, spread_p, spread, spread_fc, columns,
-        final, input_grad, out_q, out_fc, out_p, out_v,
-    ) = refs[:18]
-    weights, grads, sums = refs[18:21], refs[21:24], refs[24:27]
-    landing = dict(zip(shapes, refs[27 : 27 + len(shapes)]))
-    (
+        pad_joint, pad_fc, pad_proj, pad_small, w_joint, w_proj, in_sem, out_sem,
         in_joint, in_proj, last_q, last_fc, last_p, back_q, back_fc, back_p,
         normed, vectors, hidden_bias, qkv_t, landed, ordered, natural, out_t, log_total, att_blocks, att_t,
-        total, d_norm_two, d_middle, d_att_t, landed_back, d_out, values_natural, d_t, d_keys, d_blocks,
+        d_middle, d_att_t, landed_back, d_out, values_natural, d_t, d_keys, d_blocks,
         d_rows, d_qkv, grad_vectors, grad_hidden,
         send_sem, recv_sem, head_send, head_recv, local_sem,
-    ) = refs[27 + len(shapes) :]
+    ) = refs[len(shapes) :]
+    loads = [pltpu.make_async_copy(ins[i], loaded[i], in_sem.at[i]) for i in range(12)]
+    for i in (2, 3, 4, 5, 6, 7, 8, 9, 0, 10, 11, 1):
+        loads[i].start()
+    stores = [
+        pltpu.make_async_copy(source, outs[i], out_sem.at[i])
+        for i, source in enumerate((final, input_grad, out_q, out_fc, out_p, out_v))
+    ]
+    place_q, place_p = placing.at[:, 0:128], placing.at[:, 128:192]
+    spread, spread_fc = spreads.at[:, 0:WIDTH], spreads.at[:, WIDTH:]
     at, core = place()
     ctx = lax.axis_index("ctx")
     spot = at["x"] * 2 + core
-    is_head = ctx < HEADS
+    is_head, my_head = head_at(ctx, lax.rem(at["z"], 2))
     twin = device(at, 1 - core)
     mail = Mail(send_sem, recv_sem, twin)
 
@@ -474,6 +547,28 @@
     barrier = pltpu.get_barrier_semaphore()
     for target in known:
         pl.semaphore_signal(barrier, inc=1, device_id=target, device_id_type=MESH)
+
+    pad_joint[...] = jnp.zeros_like(pad_joint)
+    pad_fc[...] = jnp.zeros_like(pad_fc)
+    pad_proj[...] = jnp.zeros_like(pad_proj)
+    pad_small[...] = jnp.zeros_like(pad_small)
+    for i in range(2, 10):
+        loads[i].wait()
+    pad_joint[0:6, 0 : 3 * WIDTH] = raw_qkv[0].astype(F32)
+    pad_joint[0:6, 3 * WIDTH : HIDDEN] = raw_out[0].astype(F32)
+    pad_fc[0:6, :] = raw_fc[0].astype(F32)
+    reorder(pad_fc, hidden_order(), lambda t, value: pad_joint.__setitem__(
+        (slice(0, 8), slice(HIDDEN + 128 * t, HIDDEN + 128 * t + 128)), value))
+    for group in range(8):
+        for half in range(2):
+            first = HIDDEN * half + 384 * group
+            w_joint[group, :, 384 * half : 384 * half + 384] = pad_joint[:, first : first + 384].astype(BF)
+    pad_proj[0:24, :] = raw_proj[0].astype(F32)
+    for half in range(2):
+        w_proj[half] = pad_proj[:, 384 * half : 384 * half + 384].astype(BF)
+    pad_small[0:2, 0:6] = raw_gains[0].astype(F32)
+    pad_small[2:8, 0:6] = raw_biases[0].astype(F32)
+    pad_small[8:9, 0:24] = raw_fc_bias[...].astype(F32)
     pl.semaphore_wait(barrier, len(known))
 
     def group_sends(source, target):
@@ -504,17 +599,20 @@
             device_id={"ctx": peer}, device_id_type=MESH,
         )
 
+    z_lo = lax.rem(at["z"], 2)
+
     def to_heads(turn, block, out):
         for step in range(1, 16):
             peer = lax.rem(ctx + step, 16)
-
-            @pl.when(peer < HEADS)
+            has, head = head_at(peer, z_lo)
+
+            @pl.when(has)
             def _():
-                head_copy(turn, step, block.at[peer], head_span(out, ctx), peer).start()
+                head_copy(turn, step, block.at[head], head_span(out, ctx), peer).start()
 
         @pl.when(is_head)
         def _():
-            pltpu.make_async_copy(block.at[ctx], head_span(out, ctx), local_sem.at[turn]).start()
+            pltpu.make_async_copy(block.at[my_head], head_span(out, ctx), local_sem.at[turn]).start()
 
     def to_heads_received(turn, block, out):
         @pl.when(is_head)
@@ -522,46 +620,48 @@
             for step in range(1, 16):
                 source = lax.rem(ctx + 16 - step, 16)
                 head_copy(turn, step, head_span(out, source), head_span(out, source), source).wait_recv()
-            pltpu.make_async_copy(block.at[ctx], head_span(out, ctx), local_sem.at[turn]).wait()
+            pltpu.make_async_copy(block.at[my_head], head_span(out, ctx), local_sem.at[turn]).wait()
 
     def to_heads_sent(turn, block, out):
         for step in range(1, 16):
             peer = lax.rem(ctx + step, 16)
-
-            @pl.when(peer < HEADS)
+            has, head = head_at(peer, z_lo)
+
+            @pl.when(has)
             def _():
-                head_copy(turn, step, block.at[peer], head_span(out, ctx), peer).wait_send()
+                head_copy(turn, step, block.at[head], head_span(out, ctx), peer).wait_send()
 
     def from_heads(turn, blocks, out):
         @pl.when(is_head)
         def _():
             for step in range(1, 16):
                 peer = lax.rem(ctx + step, 16)
-                head_copy(turn, step, blocks.at[peer], out.at[ctx], peer).start()
-            pltpu.make_async_copy(blocks.at[ctx], out.at[ctx], local_sem.at[turn]).start()
+                head_copy(turn, step, blocks.at[peer], out.at[my_head], peer).start()
+            pltpu.make_async_copy(blocks.at[ctx], out.at[my_head], local_sem.at[turn]).start()
 
     def from_heads_received(turn, blocks, out):
         for step in range(1, 16):
             source = lax.rem(ctx + 16 - step, 16)
-
-            @pl.when(source < HEADS)
+            has, head = head_at(source, z_lo)
+
+            @pl.when(has)
             def _():
-                head_copy(turn, step, out.at[source], out.at[source], source).wait_recv()
+                head_copy(turn, step, out.at[head], out.at[head], source).wait_recv()
 
         @pl.when(is_head)
         def _():
-            pltpu.make_async_copy(blocks.at[ctx], out.at[ctx], local_sem.at[turn]).wait()
+            pltpu.make_async_copy(blocks.at[ctx], out.at[my_head], local_sem.at[turn]).wait()
 
     def from_heads_sent(turn, blocks, out):
         @pl.when(is_head)
         def _():
             for step in range(1, 16):
                 peer = lax.rem(ctx + step, 16)
-                head_copy(turn, step, blocks.at[peer], out.at[ctx], peer).wait_send()
+                head_copy(turn, step, blocks.at[peer], out.at[my_head], peer).wait_send()
 
     zl, zh = split_z(at["z"])
     waits = group_sends(w_joint, in_joint) + pair_sends(w_proj, in_proj)
-    weights[2][zl, at["y"], zh, at["x"], core] = w_small[...]
+    weights[2][zl, at["y"], zh, at["x"], core] = pad_small[...].astype(BF)
     receive(waits)
     rows = dot(place_q[...], in_joint[...].reshape(128, WIDTH)).astype(BF)
     proj_rows = dot(place_p[...], in_proj[...].reshape(64, 384)).astype(BF)
@@ -576,14 +676,16 @@
     first.straight(0)
     second.straight(0)
     first.straight(1)
+    first.ring()
+    loads[0].wait()
+    xhat, _ = normalize(x[0])
+    first.pass_on()
     second.straight(1)
-    first.ring()
-    xhat, _ = normalize(x[...])
-    first.pass_on()
-    second.ring()
     first.last()
     first.finish()
 
+    loads[10].wait()
+    loads[11].wait()
     small_rows = weights[2][...].reshape(2048, 128)
     found = jnp.zeros((16, WIDTH), F32)
     for group in range(8):
@@ -610,7 +712,7 @@
         for head in range(4):
             qkv_t[offset // 64 + head, 64 * kind : 64 * kind + 64, :] = out[64 * head : 64 * head + 64]
     to_heads(0, qkv_t, landed)
-    second.pass_on()
+    second.ring()
     to_heads_received(0, qkv_t, landed)
 
     @pl.when(is_head)
@@ -619,7 +721,7 @@
         for step in range(4):
             attend(step, ordered, natural, out_t, log_total)
 
-    second.last()
+    second.pass_on()
 
     @pl.when(is_head)
     def _():
@@ -629,16 +731,18 @@
             att_blocks[block] = position_block(lambda t: out_t[:, columns_of(t)], block).astype(BF)
 
     from_heads(1, att_blocks, att_t)
+    second.last()
     second.finish()
     from_heads_received(1, att_blocks, att_t)
 
     rows_t = att_t[...].reshape(WIDTH, 128)
     mat_out = joint_tiles(18, 6)
-    middle = x[...] + dot(flip(rows_t), mat_out) + vectors[5:6]
+    middle = x[0] + dot(flip(rows_t), mat_out) + vectors[5:6]
     xhat, factor = normalize(middle)
     normed_two = (xhat * vectors[1:2] + vectors[6:7]).astype(BF)
     normed_t = flip(normed_two)
-    gradient = cotangent[...]
+    loads[1].wait()
+    gradient = cotangent[0]
     d_two = gradient.astype(BF)
     d_norm = jnp.zeros((128, WIDTH), F32)
     twin_waits = {}
@@ -655,11 +759,11 @@
             root * (1.0 + 3 * 0.044715 * (pre * pre))
         )
         update = dot(activated, mat_proj)
-        total[...] = update if chunk == 0 else total[...] + update
+        final[...] = update if chunk == 0 else final[...] + update
         d_pre = (dot_right_t(d_two, mat_proj) * slope).astype(BF)
         grad_hidden[:, span] = sum_rows(d_pre.astype(F32))
         update = dot_right_t(d_pre, mat_fc)
-        d_norm_two[...] = update if chunk == 0 else d_norm_two[...] + update
+        input_grad[...] = update if chunk == 0 else input_grad[...] + update
         grad_fc = dot(normed_t, d_pre).astype(BF)
         grad_proj = dot_left_t(activated, d_two).astype(BF)
         for t in range(6):
@@ -667,8 +771,9 @@
             grads[1][chunk, 2 * t + 1] = grad_proj[:, columns_of(t)].reshape(2, 4, 2, 48, 128)
         key = mail.send(grads[1].at[chunk, pl.ds(6 * (1 - core), 6)], sums[1].at[chunk], twin)
         twin_waits[1, chunk] = key
-    final[...] = middle + total[...] + vectors[7:8]
-    d_norm = d_norm_two[...]
+    final[...] = middle + final[...] + vectors[7:8]
+    stores[0].start()
+    d_norm = input_grad[...]
     d_mid = gradient + norm_back(d_norm, xhat, factor, vectors[1:2])
     d_middle[...] = d_mid
     d_one = d_mid.astype(BF)
@@ -710,9 +815,9 @@
         for step in range(5, 2048 // TILE):
             attend_back(step, ordered, natural, values_natural, out_t, log_total, d_out, d_t, d_keys)
         for tile in range(16):
-            d_t[64:192, columns_of(tile)] = d_keys[columns_of(tile), :].T
+            d_t[64:192, columns_of(tile)] = d_keys[columns_of(tile), :].T.astype(BF)
         for block in range(16):
-            d_blocks[block] = position_block(lambda t: d_t[:, columns_of(t)], block).astype(BF)
+            d_blocks[block] = position_block(lambda t: d_t[:, columns_of(t)].astype(F32), block).astype(BF)
 
     from_heads(3, d_blocks, d_rows)
     back_second.collect_ring()
@@ -743,8 +848,9 @@
     for chunk in range(3):
         add_twin(0, chunk)
     back_first.ring()
-    xhat, factor = normalize(x[...])
+    xhat, factor = normalize(x[0])
     input_grad[...] = d_middle[...] + norm_back(d_norm, xhat, factor, vectors[0:1])
+    stores[1].start()
     kinds = lambda kind: sum_rows(d_qkv[:, WIDTH * kind : WIDTH * kind + WIDTH].astype(F32))
     row = lax.broadcasted_iota(jnp.int32, (16, WIDTH), 0)
     found = grad_vectors[...]
@@ -766,9 +872,9 @@
     back_second.collect(2)
     mine = [view(sums, sub, at, None) for sub in FORWARD]
     rows = jnp.concatenate([mine[t][0] for t in range(3)], axis=1)
-    last_fc[...] = dot(spread_q[...], rows).astype(BF).reshape(8, 16, 384)
+    last_fc[...] = dot_left_t(place_q[...], rows).astype(BF).reshape(8, 16, 384)
     rows = jnp.concatenate([mine[t][1] for t in range(3)], axis=1)
-    last_p[...] = dot(spread_p[...], rows).astype(BF).reshape(2, 32, 384)
+    last_p[...] = dot_left_t(place_p[...], rows).astype(BF).reshape(2, 32, 384)
     waits = group_sends(last_fc, back_fc) + pair_sends(last_p, back_p)
     mail.receive(key, sums[2])
     added(sums[2], view(grads, (2, 0), every, core))
@@ -784,25 +890,32 @@
     back_small.straight(2)
     receive(waits)
     for group in range(8):
-        out_fc[:, 384 * group : 384 * group + 384] = back_fc[group].astype(F32)[:8]
+        pad_fc[:, 384 * group : 384 * group + 384] = back_fc[group].astype(F32)[:8]
+    reorder(pad_fc, np.argsort(hidden_order()), lambda t, value: out_fc.__setitem__((ALL, columns_of(t)), value))
+    stores[3].start()
     for half in range(2):
         out_p[:, 384 * half : 384 * half + 384] = back_p[half].astype(F32)[:24]
+    stores[4].start()
     back_first.collect(1)
     back_first.straight(2)
     back_small.collect(2)
     out_v[...] = view(sums, (2, 0), at, None)[...].astype(F32)
+    stores[5].start()
     back_first.collect(2)
     rows = jnp.concatenate([view(sums, sub, at, None)[0] for sub in ATTENTION], axis=1)
-    last_q[...] = dot(spread_q[...], rows).astype(BF).reshape(8, 16, 384)
+    last_q[...] = dot_left_t(place_q[...], rows).astype(BF).reshape(8, 16, 384)
     receive(group_sends(last_q, back_q))
     for group in range(8):
         out_q[:, 384 * group : 384 * group + 384] = back_q[group].astype(F32)[:8]
+    stores[2].start()
 
     mail.finish()
     to_heads_sent(0, qkv_t, landed)
     from_heads_sent(1, att_blocks, att_t)
     to_heads_sent(2, d_att_t, landed_back)
     from_heads_sent(3, d_blocks, d_rows)
+    for store in stores:
+        store.wait()
 
 
 def place_rows(groups, rows, padded):
@@ -819,22 +932,25 @@
     return found
 
 
-def hidden_order():
-    x, group, row = np.meshgrid(np.arange(4), np.arange(16), np.arange(48), indexing="ij")
-    return (192 * group + 48 * x + row).reshape(-1)
-
-
 def local(tokens, cotangent, w_qkv, w_out, w_fc, w_proj, gains, biases, fc_bias):
-    first = jnp.concatenate([w_qkv[0], w_out[0]], axis=1).reshape(6, 8, 384)
-    hidden = jnp.transpose(w_fc[0].reshape(6, 16, 4, 48), (0, 2, 1, 3)).reshape(6, 8, 384)
-    joint = jnp.transpose(jnp.concatenate([first, hidden], axis=2), (1, 0, 2))
-    joint = jnp.pad(joint, ((0, 0), (0, 10), (0, 0)))
-    proj = jnp.pad(jnp.transpose(w_proj[0].reshape(24, 2, 384), (1, 0, 2)), ((0, 0), (0, 8), (0, 0)))
-    small = jnp.pad(jnp.concatenate([gains[0], biases[0]], axis=0), ((0, 0), (0, 122)))
-    small = jnp.concatenate([small, jnp.pad(fc_bias, ((0, 0), (0, 104))), jnp.zeros((7, 128), BF)], axis=0)
     order = hidden_order()
-    scratch = [VMEM(shape, BF) for shape in SHAPES + SHAPES + SUMS + tuple(landing_shapes().values())]
+    placing = np.concatenate([place_rows(8, 6, 16), place_rows(2, 24, 32)], axis=1)
+    spreads = np.concatenate([spread_matrix(np.arange(WIDTH), 6), spread_matrix(order, 24)], axis=1)
+    given = (tokens, cotangent, w_qkv, w_out, w_fc, w_proj, gains, biases, fc_bias)
+    given += (jnp.asarray(placing, BF), jnp.asarray(spreads, BF), jnp.asarray(order.reshape(1, HIDDEN), jnp.int32))
+    results = ((128, WIDTH), (128, WIDTH), (8, HIDDEN), (8, HIDDEN), (24, WIDTH), (16, 128))
+    scratch = [VMEM(item.shape, item.dtype) for item in given]
+    scratch += [VMEM(shape, F32) for shape in results]
+    scratch += [VMEM(shape, BF) for shape in SHAPES + SHAPES + SUMS + tuple(landing_shapes().values())]
     scratch += [
+        VMEM((16, 2 * HIDDEN), F32),
+        VMEM((8, HIDDEN), F32),
+        VMEM((32, WIDTH), F32),
+        VMEM((16, 128), F32),
+        VMEM((8, 16, WIDTH), BF),
+        VMEM((2, 32, 384), BF),
+        pltpu.SemaphoreType.DMA((12,)),
+        pltpu.SemaphoreType.DMA((6,)),
         VMEM((8, 16, WIDTH), BF),
         VMEM((2, 32, 384), BF),
         VMEM((8, 16, 384), BF),
@@ -855,13 +971,11 @@
         VMEM((16, 64, 128), BF),
         VMEM((HEADS, 64, 128), BF),
         VMEM((128, WIDTH), F32),
-        VMEM((128, WIDTH), F32),
-        VMEM((128, WIDTH), F32),
         VMEM((HEADS, 64, 128), BF),
         VMEM((64, 2048), BF),
-        VMEM((64, 2048), F32),
+        VMEM((64, 2048), BF),
         VMEM((2048, 128), BF),
-        VMEM((192, 2048), F32),
+        VMEM((192, 2048), BF),
         VMEM((2048, 128), F32),
         VMEM((16, 192, 128), BF),
         VMEM((HEADS, 192, 128), BF),
@@ -874,42 +988,44 @@
         pltpu.SemaphoreType.DMA((4, 16)),
         pltpu.SemaphoreType.DMA((4,)),
     ]
-    outs = ((128, WIDTH), (128, WIDTH), (8, HIDDEN), (8, HIDDEN), (24, WIDTH), (16, 128))
-    final, input_grad, out_q, out_fc, out_p, out_v = pl.pallas_call(
+    stay = pl.BlockSpec(memory_space=pl.ANY)
+    found = pl.pallas_call(
         layer_kernel,
-        out_shape=[jax.ShapeDtypeStruct(shape, F32) for shape in outs],
-        in_specs=[pl.BlockSpec(memory_space=VMEM)] * 12,
-        out_specs=[pl.BlockSpec(memory_space=VMEM)] * 6,
+        out_shape=[jax.ShapeDtypeStruct(shape, F32) for shape in results],
+        in_specs=[stay] * 12,
+        out_specs=[stay] * 6,
         scratch_shapes=scratch,
         compiler_params=pltpu.CompilerParams(
             collective_id=0, has_side_effects=True, vmem_limit_bytes=VMEM_LIMIT * MEGA
         ),
         name="layer",
-    )(
-        tokens[0],
-        cotangent[0],
-        joint,
-        proj,
-        small,
-        jnp.asarray(place_rows(8, 6, 16), BF),
-        jnp.asarray(place_rows(2, 24, 32), BF),
-        jnp.asarray(place_rows(8, 6, 16).T, BF),
-        jnp.asarray(place_rows(2, 24, 32).T, BF),
-        jnp.asarray(spread_matrix(np.arange(WIDTH), 6), BF),
-        jnp.asarray(spread_matrix(order, 24), BF),
-        jnp.asarray(order.reshape(1, HIDDEN), jnp.int32),
+    )(*given)
+    shapes = (
+        (128, WIDTH), (128, WIDTH), (6, 1, 3 * WIDTH), (6, 1, WIDTH), (6, 1, HIDDEN), (24, WIDTH),
+        (2, 6), (6, 1, 6), (1, 24),
     )
-    grad_fc = jnp.transpose(out_fc[:6].reshape(6, 4, 16, 48), (0, 2, 1, 3)).reshape(1, 6, HIDDEN)
+    parts = [shapes[i] for i in (2, 3, 4, 6, 7, 8)]
+    final, input_grad, qkv, out, fc, proj, d_gains, d_biases, d_fc_bias = pl.pallas_call(
+        results_kernel,
+        out_shape=[jax.ShapeDtypeStruct(shape, F32) for shape in shapes],
+        in_specs=[stay] * 6,
+        out_specs=[stay] * 9,
+        scratch_shapes=[VMEM(shape, F32) for shape in [results[2], results[3], results[5]] + parts]
+        + [pltpu.SemaphoreType.DMA((3,)), pltpu.SemaphoreType.DMA((9,))],
+        compiler_params=pltpu.CompilerParams(vmem_limit_bytes=VMEM_LIMIT * MEGA),
+        name="results",
+    )(*found)
+    rows_first = lambda value: jnp.transpose(value, (1, 0, 2))
     return (
         final[None],
         input_grad[None],
-        out_q[None, :6, : 3 * WIDTH],
-        out_q[None, :6, 3 * WIDTH :],
-        grad_fc,
-        out_p[None],
-        out_v[None, 0:2, :6],
-        out_v[None, 2:8, :6],
-        out_v[8:9, :24],
+        rows_first(qkv),
+        rows_first(out),
+        rows_first(fc),
+        proj[None],
+        d_gains[None],
+        rows_first(d_biases),
+        d_fc_bias,
     )
 
 

time: 161 us -> 168 us (1.043)
  Pallas kernels: 143 us -> 167 us
  local copies, waits for them, and re-layouts: 15 us -> 0 us
    pallas_call x0 -> x1, Pallas kernels: none -> 27.3 us  [local(): pl.pallas_call(results_kernel, out_shape=[jax.ShapeDtypeStruct(shape, F32...]
    unnamed x26 -> x0, local copies, waits for them, and re-layouts: 6.69 us -> none
    broadcast_in_dim x5 -> x0, local copies, waits for them, and re-layouts: 3.57 us -> none  [the longest x1 1.25 us: local(): out_v[None, 0:2, :6]]
    pallas_call x1, Pallas kernels: 143 us -> 140 us  [local(): pl.pallas_call(layer_kernel, out_shape=[jax.ShapeDtypeStruct(shape, F32)...]
where the time goes in v3:
time: 168 us
  Pallas kernels  167 us (99%)
    pallas_call x1, Pallas kernels, local(): pl.pallas_call(layer_kernel, out_shape=[jax.ShapeDtypeStruct(shape, F32)...  140 us
    pallas_call x1, Pallas kernels, local(): pl.pallas_call(results_kernel, out_shape=[jax.ShapeDtypeStruct(shape, F32...  27.3 us

profile of v3, /device:TPU:1, one launch (start us, length us, event | category | flops | bytes accessed | tf_op | source)
XLA Modules:
  0.0 168.0 jit_solution(3999662868715119206)
XLA Ops:
  0.6 139.9 %layer.1 = (f32[128,768]{1,0:T(8,128)}, f32[128,768]{1,0:T(8,128)}, f32[8,3072]{1,0:T(8,128)}, f32[8,3072]{1,0:T(8,128)}, f32[24,768]{1,0:T(8,128)}, /*index=5*/f32[16,128]{1,0:T(8,128)}) custom-call(f32[1,128,768]{2,1,0:T(8,128)} %refs_0_.1, f32[1,128,768]{2,1,0:T(8,128)} %refs_1_.1, bf16[1,6,2304]{2,1,0:T(8,128)(2,1)} %refs_2_.1, ...), custom_call_target="tpu_custom_call" | custom-call | tf_op jit(solution)/shard_map/layer/pallas_call | solution.py:992
  140.6 27.3 %results.1 = (f32[128,768]{1,0:T(8,128)}, f32[128,768]{1,0:T(8,128)}, f32[6,1,2304]{2,1,0:T(1,128)}, f32[6,1,768]{2,1,0:T(1,128)}, f32[6,1,3072]{2,1,0:T(1,128)}...) custom-call(f32[128,768]{1,0:T(8,128)} %get-tuple-element.24.final, ...), custom_call_target="tpu_custom_call" | custom-call | tf_op jit(solution)/shard_map/results/pallas_call | solution.py:1008

commit v4 on v3

--- a/solution.py
+++ b/solution.py
@@ -25,7 +25,8 @@
 NORM_EPS = 1e-05
 MASKED = -1e30
 MEGA = 1024 * 1024
-COPIES = 256
+COPIES = 211
+IN_FLIGHT = 48
 
 
 def place():
@@ -133,10 +134,12 @@
 
     def send(self, source, target, device_id):
         key = self.used
+        if key >= IN_FLIGHT:
+            self.sent[key - IN_FLIGHT].wait_send()
         copy = pltpu.make_async_remote_copy(
             src_ref=source,
             dst_ref=target,
-            send_sem=self.send_sem.at[key],
+            send_sem=self.send_sem.at[key % IN_FLIGHT],
             recv_sem=self.recv_sem.at[key],
             device_id=device_id,
             device_id_type=MESH,
@@ -150,16 +153,16 @@
         pltpu.make_async_remote_copy(
             src_ref=arrival,
             dst_ref=arrival,
-            send_sem=self.send_sem.at[key],
+            send_sem=self.send_sem.at[key % IN_FLIGHT],
             recv_sem=self.recv_sem.at[key],
             device_id=self.anyone,
             device_id_type=MESH,
         ).wait_recv()
 
     def finish(self):
-        for copy in self.sent:
+        for copy in self.sent[-IN_FLIGHT:]:
             copy.wait_send()
-        self.sent = []
+        assert self.used == COPIES, self.used
 
 
 class Gather:
@@ -382,15 +385,15 @@
     return slice(128 * tile, 128 * tile + 128)
 
 
-def causal(scores, first):
+def causal(scores):
     key = lax.broadcasted_iota(jnp.int32, scores.shape, 0)
-    query = lax.broadcasted_iota(jnp.int32, scores.shape, 1) + first
+    query = lax.broadcasted_iota(jnp.int32, scores.shape, 1)
     return jnp.where(key <= query, scores, MASKED)
 
 
-def scores_of(ordered, natural, first, count):
-    queries = ordered[0:64, first:count]
-    return causal(dot(natural[0:count, :], jnp.concatenate([jnp.zeros_like(queries), queries], axis=0)), first)
+def query_columns(ordered, first):
+    queries = ordered[0:64, first : first + TILE]
+    return jnp.concatenate([jnp.zeros_like(queries), queries], axis=0)
 
 
 def order_heads(landed, ordered, natural):
@@ -404,11 +407,20 @@
 def attend(step, ordered, natural, out_t, log_total):
     first = TILE * step
     count = first + TILE
-    scores = scores_of(ordered, natural, first, count)
-    best = jnp.max(scores, axis=0, keepdims=True)
-    probs = jnp.exp(scores - best)
-    total = sum_rows(probs)
-    out_t[:, first:count] = dot(ordered[128:192, 0:count], probs.astype(BF)) / total
+    queries = query_columns(ordered, first)
+    spans = [slice(first, count)] + ([slice(0, first)] if first else [])
+    scores = [dot(natural[span, :], queries) for span in spans]
+    scores[0] = causal(scores[0])
+    best = jnp.max(scores[0], axis=0, keepdims=True)
+    for part in scores[1:]:
+        best = jnp.maximum(best, jnp.max(part, axis=0, keepdims=True))
+    total = jnp.zeros((1, TILE), F32)
+    out = jnp.zeros((64, TILE), F32)
+    for span, part in zip(spans, scores):
+        probs = jnp.exp(part - best)
+        total = total + sum_rows(probs)
+        out = out + dot(ordered[128:192, span], probs.astype(BF))
+    out_t[:, first:count] = out / total
     log_total[0:1, first:count] = best + jnp.log(total)
 
 
@@ -423,8 +435,7 @@
 def attend_back(step, ordered, natural, values_natural, out_t, log_total, d_out, d_t, d_keys):
     first = TILE * step
     count = first + TILE
-    queries = ordered[0:64, first:count]
-    queries = jnp.concatenate([jnp.zeros_like(queries), queries], axis=0)
+    queries = query_columns(ordered, first)
     log_here = log_total[0:1, first:count]
     d_low = d_out[:, first:count]
     delta = sum_rows(d_low.astype(F32) * out_t[:, first:count])
@@ -434,20 +445,19 @@
     query_rows = jnp.where(low, query_rows, jnp.zeros_like(query_rows))
     d_rows = jnp.where(low, jnp.zeros_like(d_rows), d_rows)
     d_query = jnp.zeros((64, TILE), F32)
-    for begin in range(0, count, KEYS):
-        end = min(begin + KEYS, count)
+    for begin in [*range(0, first, KEYS), first]:
+        end = count if begin == first else min(begin + KEYS, first)
         scores = dot(natural[begin:end, :], queries)
-        if end == count:
-            scores = causal(scores, first - begin)
+        if begin == first:
+            scores = causal(scores)
         probs = jnp.exp(scores - log_here)
         d_scores = (probs * (dot(values_natural[begin:end, :], d_low) - delta)).astype(BF)
         d_query = d_query + dot(ordered[64:128, begin:end], d_scores)
         update = dot(d_scores, query_rows) + dot(probs.astype(BF), d_rows)
-        if begin < first:
-            done = min(end, first)
-            d_keys[begin:done, :] += update[: done - begin]
-        if end == count:
-            d_keys[first:count, :] = update[first - begin :]
+        if begin == first:
+            d_keys[begin:end, :] = update
+        else:
+            d_keys[begin:end, :] += update
     d_t[0:64, first:count] = (d_query * 0.125).astype(BF)
 
 
@@ -479,19 +489,22 @@
 def results_kernel(
     final, input_grad, joint, hidden, proj, small,
     to_final, to_input, to_qkv, to_out, to_fc, to_proj, to_gains, to_biases, to_fc_bias,
-    joint_here, hidden_here, small_here, qkv, out, fc, gains, biases, fc_bias, in_sem, out_sem,
+    final_here, input_here, joint_here, hidden_here, proj_here, small_here,
+    qkv, out, fc, gains, biases, fc_bias, in_sem, out_sem,
 ):
-    straight = [
-        pltpu.make_async_copy(source, target, out_sem.at[i])
-        for i, (source, target) in enumerate(((final, to_final), (input_grad, to_input), (proj, to_proj)))
-    ]
-    loads = [
-        pltpu.make_async_copy(source, target, in_sem.at[i])
-        for i, (source, target) in enumerate(((joint, joint_here), (hidden, hidden_here), (small, small_here)))
-    ]
-    for copy in loads + straight:
+    pairs = (
+        (joint, joint_here), (hidden, hidden_here), (small, small_here),
+        (final, final_here), (input_grad, input_here), (proj, proj_here),
+    )
+    loads = [pltpu.make_async_copy(source, target, in_sem.at[i]) for i, (source, target) in enumerate(pairs)]
+    pairs = (
+        (final_here, to_final), (input_here, to_input), (proj_here, to_proj),
+        (qkv, to_qkv), (out, to_out), (fc, to_fc), (gains, to_gains), (biases, to_biases), (fc_bias, to_fc_bias),
+    )
+    stores = [pltpu.make_async_copy(source, target, out_sem.at[i]) for i, (source, target) in enumerate(pairs)]
+    for copy in loads:
         copy.start()
-    for copy in loads:
+    for copy in loads[:3]:
         copy.wait()
     for row in range(6):
         qkv[row] = joint_here[row : row + 1, 0 : 3 * WIDTH]
@@ -500,11 +513,12 @@
         biases[row] = small_here[2 + row : 3 + row, 0:6]
     gains[...] = small_here[0:2, 0:6]
     fc_bias[...] = small_here[8:9, 0:24]
-    pairs = ((qkv, to_qkv), (out, to_out), (fc, to_fc), (gains, to_gains), (biases, to_biases), (fc_bias, to_fc_bias))
-    last = [pltpu.make_async_copy(source, target, out_sem.at[3 + i]) for i, (source, target) in enumerate(pairs)]
-    for copy in last:
+    for copy in stores[3:]:
         copy.start()
-    for copy in straight + last:
+    for load, store in zip(loads[3:], stores[:3]):
+        load.wait()
+        store.start()
+    for copy in stores:
         copy.wait()
 
 
@@ -595,7 +609,7 @@
 
     def head_copy(turn, step, source, target, peer):
         return pltpu.make_async_remote_copy(
-            source, target, head_send.at[turn, step], head_recv.at[turn, step],
+            source, target, head_send.at[turn % 2, step], head_recv.at[turn % 2, step],
             device_id={"ctx": peer}, device_id_type=MESH,
         )
 
@@ -778,6 +792,7 @@
     d_middle[...] = d_mid
     d_one = d_mid.astype(BF)
     d_att_t[...] = dot_right_t(mat_out, d_one).astype(BF).reshape(HEADS, 64, 128)
+    to_heads_sent(0, qkv_t, landed)
     to_heads(2, d_att_t, landed_back)
     grad_out = dot(rows_t, d_one).astype(BF)
     for t in range(6):
@@ -819,6 +834,7 @@
         for block in range(16):
             d_blocks[block] = position_block(lambda t: d_t[:, columns_of(t)].astype(F32), block).astype(BF)
 
+    from_heads_sent(1, att_blocks, att_t)
     from_heads(3, d_blocks, d_rows)
     back_second.collect_ring()
     back_second.straight(1)
@@ -910,8 +926,6 @@
     stores[2].start()
 
     mail.finish()
-    to_heads_sent(0, qkv_t, landed)
-    from_heads_sent(1, att_blocks, att_t)
     to_heads_sent(2, d_att_t, landed_back)
     from_heads_sent(3, d_blocks, d_rows)
     for store in stores:
@@ -982,10 +996,10 @@
         VMEM((128, 3 * WIDTH), BF),
         VMEM((16, WIDTH), F32),
         VMEM((1, HIDDEN), F32),
+        pltpu.SemaphoreType.DMA((IN_FLIGHT,)),
         pltpu.SemaphoreType.DMA((COPIES,)),
-        pltpu.SemaphoreType.DMA((COPIES,)),
-        pltpu.SemaphoreType.DMA((4, 16)),
-        pltpu.SemaphoreType.DMA((4, 16)),
+        pltpu.SemaphoreType.DMA((2, 16)),
+        pltpu.SemaphoreType.DMA((2, 16)),
         pltpu.SemaphoreType.DMA((4,)),
     ]
     stay = pl.BlockSpec(memory_space=pl.ANY)
@@ -1010,8 +1024,8 @@
         out_shape=[jax.ShapeDtypeStruct(shape, F32) for shape in shapes],
         in_specs=[stay] * 6,
         out_specs=[stay] * 9,
-        scratch_shapes=[VMEM(shape, F32) for shape in [results[2], results[3], results[5]] + parts]
-        + [pltpu.SemaphoreType.DMA((3,)), pltpu.SemaphoreType.DMA((9,))],
+        scratch_shapes=[VMEM(shape, F32) for shape in list(results) + parts]
+        + [pltpu.SemaphoreType.DMA((6,)), pltpu.SemaphoreType.DMA((9,))],
         compiler_params=pltpu.CompilerParams(vmem_limit_bytes=VMEM_LIMIT * MEGA),
         name="results",
     )(*found)

time: 168 us -> 141 us (0.84)
  Pallas kernels: 167 us -> 140 us
    pallas_call x1, Pallas kernels: 27.3 us -> 2.15 us  [local(): pl.pallas_call(results_kernel, out_shape=[jax.ShapeDtypeStruct(shape, F32...]
    pallas_call x1, Pallas kernels: 140 us -> 137 us  [local(): pl.pallas_call(layer_kernel, out_shape=[jax.ShapeDtypeStruct(shape, F32)...]
where the time goes in v4:
time: 141 us; the launch traced here: 140 us
  Pallas kernels  140 us (99%)
    pallas_call x1, Pallas kernels, local(): pl.pallas_call(layer_kernel, out_shape=[jax.ShapeDtypeStruct(shape, F32)...  137 us

profile of v4, /device:TPU:1, one launch (start us, length us, event | category | flops | bytes accessed | tf_op | source)
XLA Modules:
  0.0 140.4 jit_solution(5444245104042144282)
XLA Ops:
  0.6 137.4 %layer.1 = (f32[128,768]{1,0:T(8,128)}, f32[128,768]{1,0:T(8,128)}, f32[8,3072]{1,0:T(8,128)}, f32[8,3072]{1,0:T(8,128)}, f32[24,768]{1,0:T(8,128)}, /*index=5*/f32[16,128]{1,0:T(8,128)}) custom-call(f32[1,128,768]{2,1,0:T(8,128)} %refs_0_.1, f32[1,128,768]{2,1,0:T(8,128)} %refs_1_.1, bf16[1,6,2304]{2,1,0:T(8,128)(2,1)} %refs_2_.1, ...), custom_call_target="tpu_custom_call" | custom-call | tf_op jit(solution)/shard_map/layer/pallas_call | solution.py:1006
  138.1 2.1 %results.1 = (f32[128,768]{1,0:T(8,128)}, f32[128,768]{1,0:T(8,128)}, f32[6,1,2304]{2,1,0:T(1,128)}, f32[6,1,768]{2,1,0:T(1,128)}, f32[6,1,3072]{2,1,0:T(1,128)}...) custom-call(f32[128,768]{1,0:T(8,128)} %get-tuple-element.24.final, ...), custom_call_target="tpu_custom_call" | custom-call | tf_op jit(solution)/shard_map/results/pallas_call | solution.py:1022

commit v5 on v4

--- a/solution.py
+++ b/solution.py
@@ -118,6 +118,9 @@
         return
 
     def step(i, carry):
+        if len(terms) == 1:
+            target[i] = target[i] + terms[0][i]
+            return carry
         total = target[i].astype(F32)
         for term in terms:
             total = total + term[i].astype(F32)
@@ -794,6 +797,15 @@
     d_att_t[...] = dot_right_t(mat_out, d_one).astype(BF).reshape(HEADS, 64, 128)
     to_heads_sent(0, qkv_t, landed)
     to_heads(2, d_att_t, landed_back)
+    def add_twin(kind, chunk):
+        mail.receive(twin_waits[kind, chunk], sums[kind].at[chunk])
+        count = 3 * (kind + 1)
+        added(sums[kind].at[chunk], grads[kind].at[chunk, pl.ds(count * core, count)])
+
+    back_second = Reduce(mail, sums, landing, FORWARD, at, core)
+    for chunk in range(4):
+        add_twin(1, chunk)
+    back_second.ring()
     grad_out = dot(rows_t, d_one).astype(BF)
     for t in range(6):
         grads[0][3, t] = grad_out[:, columns_of(t)].reshape(2, 4, 2, 48, 128)
@@ -804,15 +816,6 @@
     grad_vectors[6:7] = sum_rows(d_norm)
     grad_vectors[7:8] = sum_rows(d_two.astype(F32))
 
-    def add_twin(kind, chunk):
-        mail.receive(twin_waits[kind, chunk], sums[kind].at[chunk])
-        count = 3 * (kind + 1)
-        added(sums[kind].at[chunk], grads[kind].at[chunk, pl.ds(count * core, count)])
-
-    back_second = Reduce(mail, sums, landing, FORWARD, at, core)
-    for chunk in range(4):
-        add_twin(1, chunk)
-    back_second.ring()
     add_twin(0, 3)
 
     to_heads_received(2, d_att_t, landed_back)

time: 141 us -> 140 us (level)
  no operation moved by 1% of the time
where the time goes in v5:
time: 140 us
  Pallas kernels  139 us (99%)
    pallas_call x1, Pallas kernels, local(): pl.pallas_call(layer_kernel, out_shape=[jax.ShapeDtypeStruct(shape, F32)...  137 us

profile of v5, /device:TPU:1, one launch (start us, length us, event | category | flops | bytes accessed | tf_op | source)
XLA Modules:
  0.0 140.3 jit_solution(9823228422047616358)
XLA Ops:
  0.6 137.3 %layer.1 = (f32[128,768]{1,0:T(8,128)}, f32[128,768]{1,0:T(8,128)}, f32[8,3072]{1,0:T(8,128)}, f32[8,3072]{1,0:T(8,128)}, f32[24,768]{1,0:T(8,128)}, /*index=5*/f32[16,128]{1,0:T(8,128)}) custom-call(f32[1,128,768]{2,1,0:T(8,128)} %refs_0_.1, f32[1,128,768]{2,1,0:T(8,128)} %refs_1_.1, bf16[1,6,2304]{2,1,0:T(8,128)(2,1)} %refs_2_.1, ...), custom_call_target="tpu_custom_call" | custom-call | tf_op jit(solution)/shard_map/layer/pallas_call | solution.py:1009
  138.0 2.1 %results.1 = (f32[128,768]{1,0:T(8,128)}, f32[128,768]{1,0:T(8,128)}, f32[6,1,2304]{2,1,0:T(1,128)}, f32[6,1,768]{2,1,0:T(1,128)}, f32[6,1,3072]{2,1,0:T(1,128)}...) custom-call(f32[128,768]{1,0:T(8,128)} %get-tuple-element.24.final, ...), custom_call_target="tpu_custom_call" | custom-call | tf_op jit(solution)/shard_map/results/pallas_call | solution.py:1025
